TPU v7x, 256 devices: a whole 4x4x8 slice. The times are simulated.
256 devices in a mesh: grp: 2 (over core), seq: 32 (over x, z), tp: 4 (over y).
Axes of the slice: x: 4, y: 4, z: 8, core: 2. Of those that a mesh axis runs over, the one named last changes fastest.
Arguments:
- neighbour_states: bfloat16 [64, 4, 128, 896], P('seq', 'tp'), may hold values from -64 to 64
- queries: bfloat16 [4096, 8192], P('seq', 'tp'), may hold values from -400 to 400
- out_grad: bfloat16 [4096, 8192], P('seq', 'tp'), may hold values from -6 to 6
- kv_weight: bfloat16 [2, 896, 8192], P('grp', None, 'tp'), may hold values from -0.1875 to 0.1875
- counts: int32 [64], replicated, may hold values from 0 to 4, as said below
- token_mask: int32 [64, 4, 128], replicated, may hold values from 0 to 1, as said below
Outputs:
- kv_grad: float32 [2, 896, 8192], P('grp', 'seq', 'tp')
Inputs may be any that keep to these rules, and one draw needn't show every extreme that they name: `counts`: stretch 0 retrieves none, the last stretch 4, and every stretch c with c % 2 = 1 at least one. `token_mask`: in each neighbour block the ones form a prefix of 1 to 128 tokens.
All inputs are finite; a program needn't handle non-finite values.
Results may differ from a plain program's by a relative error of at most 0.0065.
The roundings to bfloat16 on the way count: a program that leaves them out, or rounds other values in their place, can miss the bound.
Values may be sent and summed in bfloat16 or wider, within the bound.
A program may use at most 128 MiB of HBM per device.

v0:
```python
import jax
import jax.numpy as jnp
from jax import lax
from jax.sharding import PartitionSpec as P

HD = 128
SLOTS = 4
NLEN = 128
STRETCH = 64


eps = 1e-06


def shifted_2(block, axis, distance):
    devices = range(lax.axis_size(axis))
    route = [(i - distance, i) for i in devices if i - distance in devices]
    return lax.ppermute(block, axis, route)


def normalize(states):
    values_f = states.astype(jnp.float32)
    mean_sq = jnp.mean(values_f * values_f, axis=-1, keepdims=True)
    return (values_f * lax.rsqrt(mean_sq + eps)).astype(jnp.bfloat16)


def key_valid(counts, token_mask):
    slot_ids = jnp.arange(SLOTS, dtype=jnp.int32)
    alive = (slot_ids[None, :] < counts[:, None])[:, :, None] & (token_mask > 0)
    return alive.reshape(counts.shape[0], SLOTS * NLEN)


def attend_back(query_tiles, key_tiles, value_tiles, out_tiles, live_keys):
    inv_root = HD ** (-0.5)
    scores = (
        jnp.einsum("cqhd,ckhd->chqk", query_tiles, key_tiles, preferred_element_type=jnp.float32)
        * inv_root
    )
    key_mask = live_keys[:, None, None, :]
    row_top = jnp.max(jnp.where(key_mask, scores, -1000000000.0), axis=-1, keepdims=True)
    exponent = jnp.exp(jnp.where(key_mask, scores - row_top, -jnp.inf))
    row_total = jnp.maximum(jnp.sum(exponent, axis=-1, keepdims=True), 1.0)
    attn_probs = exponent / row_total
    probs_low = attn_probs.astype(jnp.bfloat16)
    value_grads = jnp.einsum(
        "chqk,cqhd->ckhd", probs_low, out_tiles, preferred_element_type=jnp.float32
    ).astype(jnp.bfloat16)
    prob_grads = jnp.einsum(
        "cqhd,ckhd->chqk", out_tiles, value_tiles, preferred_element_type=jnp.float32
    )
    row_delta = jnp.sum(prob_grads * attn_probs, axis=-1, keepdims=True)
    score_grads = (attn_probs * (prob_grads - row_delta) * inv_root).astype(jnp.bfloat16)
    key_grads = jnp.einsum(
        "chqk,cqhd->ckhd", score_grads, query_tiles, preferred_element_type=jnp.float32
    ).astype(jnp.bfloat16)
    return (key_grads, value_grads)


def project_rows(normed, weight):
    flat_rows = normed.reshape(-1, normed.shape[-1])
    result = jnp.dot(flat_rows, weight, preferred_element_type=jnp.float32).astype(jnp.bfloat16)
    return result.reshape(normed.shape[:-1] + (weight.shape[1],))


def per_device(neighbour_states, queries, out_grad, kv_weight, counts, token_mask):
    group_role = lax.axis_index("grp")
    seq_index = lax.axis_index("seq")
    stretches_here = queries.shape[0] // STRETCH
    head_cols = queries.shape[1]
    local_heads = head_cols // HD
    key_rows = SLOTS * NLEN
    own_weight = kv_weight[0]
    gathered = lax.all_gather(normalize(neighbour_states), "tp", axis=1, tiled=True)
    normed = gathered.reshape(stretches_here, key_rows, gathered.shape[-1])
    weight_stack = (own_weight,)
    projected = jnp.stack([project_rows(normed, weight) for weight in weight_stack])
    earlier_proj = shifted_2(projected[:, -1], "seq", 1)
    key_block = jnp.concatenate([earlier_proj[:, None], projected[:, :-1]], 1)
    key_tiles = shifted_2(key_block[0], "grp", 1)
    value_tiles = key_block[0]
    alive = key_valid(counts, token_mask)
    shifted = jnp.concatenate([jnp.zeros((1, key_rows), dtype=bool), alive[:-1]], 0)
    live_keys = lax.dynamic_slice_in_dim(shifted, seq_index * stretches_here, stretches_here, 0)

    def decode():
        key_grads, value_grads = attend_back(
            queries.reshape(stretches_here, STRETCH, local_heads, HD),
            key_tiles.reshape(stretches_here, key_rows, local_heads, HD),
            value_tiles.reshape(stretches_here, key_rows, local_heads, HD),
            out_grad.reshape(stretches_here, STRETCH, local_heads, HD),
            live_keys,
        )
        return (
            key_grads.reshape(stretches_here, key_rows, head_cols),
            value_grads.reshape(stretches_here, key_rows, head_cols),
        )

    def nothing():
        zeros_tile = jnp.zeros((stretches_here, key_rows, head_cols), jnp.bfloat16)
        return (zeros_tile, zeros_tile)

    key_grads, value_grads = lax.cond(group_role == 1, decode, nothing)
    returned = shifted_2((key_grads[0], value_grads[0]), "seq", -1)
    grads_keys = jnp.concatenate([key_grads[1:], returned[0][None]], 0)
    grads_values = jnp.concatenate([value_grads[1:], returned[1][None]], 0)
    flat_states = normed.reshape(stretches_here * key_rows, -1)
    dims = (((0,), (0,)), ((), ()))
    received = shifted_2(grads_keys, "grp", -1)
    own_grads = jnp.where(group_role == 0, received, grads_values).reshape(
        stretches_here * key_rows, head_cols
    )
    summed = lax.psum_scatter(
        lax.dot_general(flat_states, own_grads, dims, preferred_element_type=jnp.float32),
        "seq",
        scatter_dimension=0,
        tiled=True,
    )
    return summed[None]


def solution(mesh):
    return jax.shard_map(
        per_device,
        mesh=mesh,
        in_specs=(
            P("seq", "tp", None, None),
            P("seq", "tp"),
            P("seq", "tp"),
            P("grp", None, "tp"),
            P(),
            P(),
        ),
        out_specs=P("grp", "seq", "tp"),
        check_vma=False,
    )
```

profile of v0, /device:TPU:1, one launch (start us, length us, event | category | flops | bytes accessed | tf_op | source)
XLA Modules:
  0.0 395.0 jit_solution(5592719230634218601)
XLA Ops:
  9.7 35.2 %all-gather.2.cloned.1.call-done = bf16[2,4,128,896]{3,2,1,0:T(8,128)(2,1)} async-done(((bf16[2,1,128,896]{3,2,1,0:T(8,128)(2,1)}), bf16[2,4,128,896]{3,2,1,0:T(8,128)(2,1)}) %all-gather.2.cloned.1.call-update) | async-done | bytes 1835024 | tf_op jit(solution)/shard_map/all_gather | solution.py:73
  44.9 7.1 %convolution_convert_fusion.1 = bf16[1024,2048]{1,0:T(8,128)(2,1)S(1)} fusion(bf16[1024,896]{1,0:T(8,128)(2,1)} %bitcast.70, bf16[1,896,2048]{2,1,0:T(8,128)(2,1)} %param.11), kind=kOutput, calls=%fused_computation.39 | convolution fusion | flops 3760193536 | bytes 9699328 | tf_op jit(solution)/shard_map/dot_general | solution.py:61
  52.6 3.3 collective-permute-start
  55.9 44.1 %collective-permute-done = bf16[1,512,2048]{2,1,0:T(8,128)(2,1)S(1)} collective-permute-done((bf16[1,512,2048]{2,1,0:T(8,128)(2,1)S(1)}, bf16[1,512,2048]{2,1,0:T(8,128)(2,1)S(1)}, u32[]{:S(2)}, u32[]{:S(2)}) %collective-permute-start) | collective-permute-done | bytes 2097184 | tf_op jit(solution)/shard_map/ppermute | solution.py:18
  100.1 3.5 pad_maximum_fusion
  104.9 8.5 %collective-permute-done.1 = bf16[2,512,2048]{2,1,0:T(8,128)(2,1)} collective-permute-done((bf16[2,512,2048]{2,1,0:T(8,128)(2,1)}, bf16[2,512,2048]{2,1,0:T(8,128)(2,1)}, u32[]{:S(2)}, u32[]{:S(2)}) %collective-permute-start.1) | collective-permute-done | bytes 4194336 | tf_op jit(solution)/shard_map/ppermute | solution.py:18
  113.4 36.3 %conditional.1 = (bf16[2,512,2048]{1,2,0:T(8,128)(2,1)}, bf16[2,512,2048]{1,2,0:T(8,128)(2,1)}) conditional(s32[]{:T(128)} %convert_element_type.32, () %tuple.13, (s32[64,4]{1,0:T(8,128)S(1)}, bf16[128,2048]{1,0:T(8,128)(2,1)S(1)}, bf16[2,512,2048]{2,1,0:T(8,128)(2,1)}, bf16[128,2048]{1,0:T(8,128)(2,1)S(1)}, ...), branch_computations={%region_1.0_spmd, %region_2.6_spmd.clone.clone} | conditional | flops 1093734656 | bytes 75866464 | solution.py:102
  114.1 3.8 fusion.3
  117.9 3.1 fusion.39
  122.5 4.0 %fusion.6 = f32[2,16,64,512]{3,2,1,0:T(8,128)} fusion(bf16[2,512,16,128]{3,2,1,0:T(8,128)(2,1)S(1)} %bitcast.56, bf16[2,64,16,128]{3,2,1,0:T(8,128)(2,1)S(1)} %bitcast.61), kind=kOutput, calls=%fused_computation.5 | convolution fusion | flops 268435456 | bytes 8912896 | tf_op jit(solution)/shard_map/cond/branch_1_fun/cqhd,ckhd->chqk/dot_general | solution.py:48
  126.5 17.8 %fusion.18 = bf16[2,16,512,128]{2,3,1,0:T(8,128)(2,1)} fusion(f32[2,16,64,512]{3,2,1,0:T(8,128)} %fusion.6, bf16[2,64,16,128]{3,2,1,0:T(8,128)(2,1)S(1)} %bitcast.60, f32[2,16,64,512]{3,2,1,0:T(8,128)} %get-tuple-element.103, f32[2,16,64]{2,1,0:T(8,128)S(1)} %broadcast_maximum_fusion), kind=kOutput, calls=%fused_computation.16 | convolution fusion | flops 277875200 | bytes 13115392 | tf_op jit(solution)/shard_map/cond/branch_1_fun/chqk,cqhd->ckhd/dot_general | solution.py:53
  144.3 5.5 %convolution_convert_fusion = bf16[2,16,512,128]{2,3,1,0:T(8,128)(2,1)} fusion(bf16[2,64,16,128]{3,2,1,0:T(8,128)(2,1)S(1)} %bitcast.62, f32[2,16,64,512]{3,2,1,0:T(8,128)} %get-tuple-element.103, f32[2,16,64]{2,1,0:T(8,128)S(1)} %broadcast_maximum_fusion), kind=kOutput, calls=%fused_computation.15 | convolution fusion | flops 272629760 | bytes 8921088 | tf_op jit(solution)/shard_map/cond/branch_1_fun/chqk,cqhd->ckhd/dot_general | solution.py:45
  149.8 6.3 %copy.39 = bf16[2,512,2048]{2,1,0:T(8,128)(2,1)} copy(bf16[2,512,2048]{1,2,0:T(8,128)(2,1)} %get-tuple-element.22) | data formatting | bytes 8388608 | tf_op jit(solution)/shard_map/cond | solution.py:102
  156.0 2.6 fusion.41
  159.9 38.6 %collective-permute-done.2 = bf16[512,2048]{1,0:T(8,128)(2,1)S(1)} collective-permute-done((bf16[512,2048]{1,0:T(8,128)(2,1)S(1)}, bf16[512,2048]{1,0:T(8,128)(2,1)S(1)}, u32[]{:S(2)}, u32[]{:S(2)}) %collective-permute-start.2) | collective-permute-done | bytes 2097184 | tf_op jit(solution)/shard_map/ppermute | solution.py:18
  200.9 3.3 collective-permute-start.3
  204.1 6.3 %copy.41 = bf16[2,512,2048]{2,1,0:T(8,128)(2,1)} copy(bf16[2,512,2048]{1,2,0:T(8,128)(2,1)} %get-tuple-element.23) | data formatting | bytes 8388608 | tf_op jit(solution)/shard_map/cond | solution.py:102
  210.4 4.0 %fusion.40 = (bf16[1,512,2048]{2,1,0:T(8,128)(2,1)S(1)}, bf16[512,2048]{1,0:T(8,128)(2,1)}) fusion(bf16[2,512,2048]{2,1,0:T(8,128)(2,1)} %copy.41), kind=kLoop, calls=%fused_computation.52 | loop fusion | bytes 8388608 | tf_op jit(solution)/shard_map/slice | solution.py:105
  215.9 39.3 %collective-permute-done.4 = bf16[512,2048]{1,0:T(8,128)(2,1)} collective-permute-done((bf16[512,2048]{1,0:T(8,128)(2,1)}, bf16[512,2048]{1,0:T(8,128)(2,1)}, u32[]{:S(2)}, u32[]{:S(2)}) %collective-permute-start.4) | collective-permute-done | bytes 2097184 | tf_op jit(solution)/shard_map/ppermute | solution.py:18
  257.4 6.0 %fusion.42 = f32[896,2048]{1,0:T(8,128)} fusion(bf16[1024,896]{1,0:T(8,128)(2,1)S(1)} %bitcast.71, bf16[1024,2048]{1,0:T(8,128)(2,1)S(1)} %bitcast.57), kind=kOutput, calls=%fused_computation.54 | convolution fusion | flops 3758096384 | bytes 13369344 | tf_op jit(solution)/shard_map/dot_general | solution.py:113
  263.4 101.3 %fusion = f32[32,2048]{1,0:T(8,128)S(1)} fusion(f32[896,2048]{1,0:T(8,128)} %fusion.42), kind=kCustom, calls=%all-reduce-scatter | all-reduce-scatter fusion | flops 2097153 | bytes 7603200
  367.9 5.1 %collective-permute-start.7 = (f32[32,2048]{1,0:T(8,128)S(1)}, f32[32,2048]{1,0:T(8,128)S(1)}, u32[]{:S(2)}, u32[]{:S(2)}) collective-permute-start(f32[32,2048]{1,0:T(8,128)S(1)} %fusion), channel_id=1, source_target_pairs={{0,12},{4,16},{8,20},{12,24},{16,28},{20,32},{24,36},{28,40},{32,4... | collective-permute-start | bytes 786440
  373.0 6.4 %collective-permute-start.8 = (f32[28,2048]{1,0:T(8,128)S(1)}, f32[28,2048]{1,0:T(8,128)S(1)}, u32[]{:S(2)}, u32[]{:S(2)}) collective-permute-start(f32[28,2048]{1,0:T(8,128)S(1)} %slice.46), channel_id=1, source_target_pairs={{0,16},{4,20},{8,24},{12,28},{16,32},{20,36},{24,40},{28,44},{32,4... | collective-permute-start | bytes 688136
  380.6 5.7 %collective-permute-done.8 = f32[28,2048]{1,0:T(8,128)S(1)} collective-permute-done((f32[28,2048]{1,0:T(8,128)S(1)}, f32[28,2048]{1,0:T(8,128)S(1)}, u32[]{:S(2)}, u32[]{:S(2)}) %collective-permute-start.8) | collective-permute-done | bytes 229408
  (46 shorter events, 19.8 us)
Async XLA Ops:
  6.5 38.4 %all-gather.2.cloned.1.call-start = ((), (), s32[]{:S(2)}) async-start(), calls=%async_computation | async-start | bytes 2293760 | tf_op jit(solution)/shard_map/all_gather | solution.py:73
  52.6 47.5 %collective-permute-start = (bf16[1,512,2048]{2,1,0:T(8,128)(2,1)S(1)}, bf16[1,512,2048]{2,1,0:T(8,128)(2,1)S(1)}, u32[]{:S(2)}, u32[]{:S(2)}) collective-permute-start(bf16[1,512,2048]{2,1,0:T(8,128)(2,1)S(1)} %get-tuple-element.110), channel_id=1, source_target_pairs={{0,4},{4,8},{8,12},{12,16},{16,20},{20,24},{24,28},{28,32},{32,36}... | collective-permute-start | bytes 6291464 | tf_op jit(solution)/shard_map/ppermute | solution.py:18
  100.1 13.3 %copy-start.1 = (bf16[128,2048]{1,0:T(8,128)(2,1)S(1)}, bf16[128,2048]{1,0:T(8,128)(2,1)}, u32[]{:S(2)}) copy-start(bf16[128,2048]{1,0:T(8,128)(2,1)} %param.9) | copy-start | bytes 1572868
  100.1 13.3 %copy-start.2 = (bf16[128,2048]{1,0:T(8,128)(2,1)S(1)}, bf16[128,2048]{1,0:T(8,128)(2,1)}, u32[]{:S(2)}) copy-start(bf16[128,2048]{1,0:T(8,128)(2,1)} %param.10) | copy-start | bytes 1572868
  100.1 13.4 %copy-start.3 = (s32[64,4,128]{2,1,0:T(4,128)S(1)}, s32[64,4,128]{2,1,0:T(4,128)}, u32[]{:S(2)}) copy-start(s32[64,4,128]{2,1,0:T(4,128)} %param.13) | copy-start | bytes 393220
  100.1 13.4 %copy-start.4 = (s32[64]{0:T(128)S(1)}, s32[64]{0:T(128)}, u32[]{:S(2)}) copy-start(s32[64]{0:T(128)} %param.12) | copy-start | bytes 772
  103.6 9.8 %collective-permute-start.1 = (bf16[2,512,2048]{2,1,0:T(8,128)(2,1)}, bf16[2,512,2048]{2,1,0:T(8,128)(2,1)}, u32[]{:S(2)}, u32[]{:S(2)}) collective-permute-start(bf16[2,512,2048]{2,1,0:T(8,128)(2,1)} %get-tuple-element.109), channel_id=1, source_target_pairs={{0,128},{1,129},{2,130},{3,131},{4,132},{5,133},{6,134},{7,135},{8... | collective-permute-start | bytes 12582920 | tf_op jit(solution)/shard_map/ppermute | solution.py:18
  117.9 3.2 copy-start
  158.7 39.9 %collective-permute-start.2 = (bf16[512,2048]{1,0:T(8,128)(2,1)S(1)}, bf16[512,2048]{1,0:T(8,128)(2,1)S(1)}, u32[]{:S(2)}, u32[]{:S(2)}) collective-permute-start(bf16[512,2048]{1,0:T(8,128)(2,1)S(1)} %get-tuple-element.107), channel_id=1, source_target_pairs={{4,0},{8,4},{12,8},{16,12},{20,16},{24,20},{28,24},{32,28},{36,32}... | collective-permute-start | bytes 6291464 | tf_op jit(solution)/shard_map/ppermute | solution.py:18
  200.9 54.4 %collective-permute-start.3 = (bf16[2,512,2048]{2,1,0:T(8,128)(2,1)}, bf16[2,512,2048]{2,1,0:T(8,128)(2,1)}, u32[]{:S(2)}, u32[]{:S(2)}) collective-permute-start(bf16[2,512,2048]{2,1,0:T(8,128)(2,1)} %pad_maximum_fusion.1), channel_id=1, source_target_pairs={{128,0},{129,1},{130,2},{131,3},{132,4},{133,5},{134,6},{135,7},{1... | collective-permute-start | bytes 12582920 | tf_op jit(solution)/shard_map/ppermute | solution.py:18
  214.4 40.8 %collective-permute-start.4 = (bf16[512,2048]{1,0:T(8,128)(2,1)}, bf16[512,2048]{1,0:T(8,128)(2,1)}, u32[]{:S(2)}, u32[]{:S(2)}) collective-permute-start(bf16[512,2048]{1,0:T(8,128)(2,1)} %get-tuple-element.105), channel_id=1, source_target_pairs={{4,0},{8,4},{12,8},{16,12},{20,16},{24,20},{28,24},{32,28},{36,32}... | collective-permute-start | bytes 6291464 | tf_op jit(solution)/shard_map/ppermute | solution.py:18
  255.2 2.1 copy-start.6
  263.3 116.0 %copy-start.5 = (u32[256]{0:T(256)S(1)}, u32[256]{0:T(256)}, u32[]{:S(2)}) copy-start(u32[256]{0:T(256)} %constant.49) | copy-start | bytes 3076
  364.7 21.6 %collective-permute-start.5 = (f32[32,2048]{1,0:T(8,128)S(1)}, f32[32,2048]{1,0:T(8,128)S(1)}, u32[]{:S(2)}, u32[]{:S(2)}) collective-permute-start(f32[32,2048]{1,0:T(8,128)S(1)} %fusion), channel_id=1, source_target_pairs={{0,4},{4,8},{8,12},{12,16},{16,20},{20,24},{24,28},{28,32},{32,36}... | collective-permute-start | bytes 786440
  366.1 20.2 %collective-permute-start.6 = (f32[32,2048]{1,0:T(8,128)S(1)}, f32[32,2048]{1,0:T(8,128)S(1)}, u32[]{:S(2)}, u32[]{:S(2)}) collective-permute-start(f32[32,2048]{1,0:T(8,128)S(1)} %fusion), channel_id=1, source_target_pairs={{0,8},{4,12},{8,16},{12,20},{16,24},{20,28},{24,32},{28,36},{32,40... | collective-permute-start | bytes 786440
  367.9 18.5 %collective-permute-start.7 = (f32[32,2048]{1,0:T(8,128)S(1)}, f32[32,2048]{1,0:T(8,128)S(1)}, u32[]{:S(2)}, u32[]{:S(2)}) collective-permute-start(f32[32,2048]{1,0:T(8,128)S(1)} %fusion), channel_id=1, source_target_pairs={{0,12},{4,16},{8,20},{12,24},{16,28},{20,32},{24,36},{28,40},{32,4... | collective-permute-start | bytes 786440
  373.0 13.4 %collective-permute-start.8 = (f32[28,2048]{1,0:T(8,128)S(1)}, f32[28,2048]{1,0:T(8,128)S(1)}, u32[]{:S(2)}, u32[]{:S(2)}) collective-permute-start(f32[28,2048]{1,0:T(8,128)S(1)} %slice.46), channel_id=1, source_target_pairs={{0,16},{4,20},{8,24},{12,28},{16,32},{20,36},{24,40},{28,44},{32,4... | collective-permute-start | bytes 688136
Sparse Core Ops, SparseCore 0:
  9.8 35.0 all-gather.1
where the time goes:
time: 402 us; the launch traced here: 395 us
  waiting for transfers between devices  171 us (43%)
  blocking collectives  101 us (25%)
  matrix products  44.1 us (11%)
  starting transfers between devices  25.3 us (6%)
  local copies, waits for them, and re-layouts  24 us (6%)
  other arithmetic  14.3 us (4%)
  between operations  14.2 us (4%)
    ppermute x5, waiting for transfers between devices, shifted_2(): return lax.ppermute(block, axis, route)  131 us
    unnamed x1, blocking collectives  101 us
    all_gather x1, waiting for transfers between devices, per_device(): lax.all_gather(normalize(neighbour_states), 'tp', axis=1, tiled=True)  35.2 us
    dot_general x1, matrix products, attend_back(): jnp.einsum('chqk,cqhd->ckhd', score_grads, query_tiles, preferred_element...  17.8 us
    unnamed x4, starting transfers between devices  14.6 us
    cond x2, local copies, waits for them, and re-layouts, per_device(): key_grads, value_grads = lax.cond(group_role == 1, decode, nothing)  12.6 us
    ppermute x5, starting transfers between devices, shifted_2(): return lax.ppermute(block, axis, route)  10.6 us
  transfers between devices with their start and end apart: 10, of which 6 were waited for; matrix products, arithmetic and copies ran while one was open for 3% of the time, Pallas kernels for 0%

commit v1 on v0

v1 whole, which is shorter than its diff:
```python
import jax
import jax.numpy as jnp
from jax import lax
from jax.experimental import pallas as pl
from jax.experimental.pallas import tpu as pltpu
from jax.sharding import PartitionSpec as P

HD = 128
SLOTS = 4
NLEN = 128
STRETCH = 64
E = 896
ROWS = 28
PAD = 32
XS, ZS, TP = 4, 8, 4
SEQ = XS * ZS
COLS = 1024
PAIR = 2 * HD
PAIRS = COLS // PAIR
KEYS = SLOTS * NLEN
XC = 5
ZC = 3
EPS = 1e-06
CODED = False
WIRE = jnp.bfloat16 if CODED else jnp.float32
F32 = jnp.float32
BF16 = jnp.bfloat16
MESH = pl.DeviceIdType.MESH
FIRST, SECOND = slice(0, HD), slice(HD, 2 * HD)


def chains(size):
    far = size // 2
    found, start = [], 0
    for direction, half, steps in (
        (1, SECOND, far), (1, FIRST, far - 1), (-1, FIRST, far), (-1, SECOND, far - 1)
    ):
        found.append((direction, half, steps, start))
        start += steps
    return found


def encode(block):
    return block


def decode(message):
    return message


def kernel(
    counts, token_mask, states, queries, out_grad, weight, out,
    normed, weights, query_rows, grad_rows, chooser, turned, key_grads, value_grads, live,
    partial, sent_x, got_x, sent_z, got_z, mid_z, mid_x,
    sent_z2, got_z2, sent_x2, got_x2, final, swapped,
    local_sem, gs, gr, sx, rx, sz, rz, sz2, rz2, sx2, rx2,
):
    g = lax.axis_index("grp")
    s = lax.axis_index("seq")
    t = lax.axis_index("tp")
    x, z = lax.div(s, ZS), lax.rem(s, ZS)
    other = 1 - g
    t_up, t_down, t_far = lax.rem(t + 1, TP), lax.rem(t + TP - 1, TP), lax.rem(t + 2, TP)
    x_up = (g, lax.rem(x + 1, XS) * ZS + z, t)
    x_down = (g, lax.rem(x + XS - 1, XS) * ZS + z, t)
    z_up = (g, x * ZS + lax.rem(z + 1, ZS), t)
    z_down = (g, x * ZS + lax.rem(z + ZS - 1, ZS), t)
    s_up = (g, lax.rem(s + 1, SEQ), t)
    s_down = (g, lax.rem(s + SEQ - 1, SEQ), t)
    y_up, y_down, mate = (g, s, t_up), (g, s, t_down), (other, s, t)

    barrier = pltpu.get_barrier_semaphore()
    everyone = (mate, y_up, y_down, x_up, x_down, z_up, z_down, s_up, s_down)
    for device in everyone:
        pl.semaphore_signal(barrier, inc=1, device_id=device, device_id_type=MESH)

    own_cols = pl.ds(pl.multiple_of(g * COLS, COLS), COLS)
    mate_cols = pl.ds(pl.multiple_of(other * COLS, COLS), COLS)
    locals_ = [
        pltpu.make_async_copy(weight.at[0, :, own_cols], weights.at[g], local_sem.at[0]),
        pltpu.make_async_copy(
            queries.at[pl.ds(STRETCH, STRETCH), own_cols], query_rows.at[0], local_sem.at[1]
        ),
        pltpu.make_async_copy(
            out_grad.at[pl.ds(STRETCH, STRETCH), own_cols], grad_rows.at[0], local_sem.at[2]
        ),
    ]
    for copy in locals_:
        copy.start()

    for i in range(2):
        rows = states[i, 0].astype(F32)
        mean_sq = jnp.mean(rows * rows, axis=-1, keepdims=True)
        normed[i, t] = (rows * lax.rsqrt(mean_sq + EPS)).astype(BF16)

    pl.semaphore_wait(barrier, len(everyone))

    def remote(src, dst, index, device):
        return pltpu.make_async_remote_copy(
            src_ref=src, dst_ref=dst, send_sem=gs.at[index], recv_sem=gr.at[index],
            device_id=device, device_id_type=MESH,
        )

    low, high = pl.ds(0, NLEN // 2), pl.ds(NLEN // 2, NLEN // 2)
    mine = normed.at[g, t]
    below, above = normed.at[g, t_down], normed.at[g, t_up]
    far_low, far_high = normed.at[g, t_far, low], normed.at[g, t_far, high]
    to_up = remote(mine, mine, 0, y_up)
    to_down = remote(mine, mine, 1, y_down)
    to_up.start()
    to_down.start()
    weight_swap = remote(weight.at[0, :, mate_cols], weights.at[g], 8, mate)
    weight_swap.start()
    shift_q = remote(queries.at[pl.ds(0, STRETCH), own_cols], query_rows.at[1], 9, s_down)
    shift_g = remote(out_grad.at[pl.ds(0, STRETCH), own_cols], grad_rows.at[1], 10, s_down)
    shift_q.start()
    shift_g.start()

    def choose(b, carry):
        feature = lax.broadcasted_iota(jnp.int32, (PAD, E), 1)
        row = lax.broadcasted_iota(jnp.int32, (PAD, E), 0)
        hit = (feature - row == b * ROWS) & (row < ROWS)
        at = pl.ds(pl.multiple_of(b * PAD, PAD), PAD)
        chooser[at, :] = jnp.where(hit, 1.0, 0.0).astype(BF16)
        return carry

    lax.fori_loop(0, SEQ, choose, 0)

    for i in range(2):
        c = 2 * s + i
        count = jnp.where(c == 2 * SEQ - 1, 0, counts[c])
        lengths = jnp.sum(token_mask[c].astype(F32), axis=1, keepdims=True)
        token = lax.broadcasted_iota(jnp.int32, (NLEN, HD), 0).astype(F32)
        for j in range(SLOTS):
            bound = lengths[j : j + 1, :] * jnp.where(j < count, 1.0, 0.0)
            live[i, j * NLEN : (j + 1) * NLEN, :] = jnp.where(token < bound, 1.0, 0.0)

    def turn(slot):
        for i in range(2):
            at = pl.ds(pl.multiple_of(i * KEYS + slot * NLEN, NLEN), NLEN)
            turned[:, at] = lax.dot_general(
                chooser[...], normed[i, slot], (((1,), (1,)), ((), ())),
                preferred_element_type=F32,
            ).astype(BF16)

    turn_slot = lambda n, carry: (turn(lax.rem(t + n, TP)), carry)[1]

    remote(below, below, 0, y_down).wait_recv()
    up_half = remote(normed.at[g, t_down, low], normed.at[g, t_down, low], 2, y_up)
    up_half.start()
    mate_below = remote(below, below, 4, mate)
    mate_below.start()
    remote(above, above, 1, y_up).wait_recv()
    down_half = remote(normed.at[g, t_up, high], normed.at[g, t_up, high], 3, y_down)
    down_half.start()
    mate_above = remote(above, above, 5, mate)
    mate_above.start()
    turn(t)
    remote(far_low, far_low, 2, y_down).wait_recv()
    mate_far_low = remote(far_low, far_low, 6, mate)
    mate_far_low.start()
    remote(far_high, far_high, 3, y_up).wait_recv()
    mate_far_high = remote(far_high, far_high, 7, mate)
    mate_far_high.start()
    remote(normed.at[other, t_down], normed.at[other, t_down], 4, mate).wait_recv()
    remote(normed.at[other, t_up], normed.at[other, t_up], 5, mate).wait_recv()
    remote(normed.at[other, t_far, low], normed.at[other, t_far, low], 6, mate).wait_recv()
    remote(normed.at[other, t_far, high], normed.at[other, t_far, high], 7, mate).wait_recv()
    lax.fori_loop(1, TP, turn_slot, 0)
    for copy in locals_:
        copy.wait()
    remote(weight.at[0, :, mate_cols], weights.at[other], 8, mate).wait_recv()
    shift_q.wait_recv()
    shift_g.wait_recv()

    def message(sent, got, ssem, rsem, lead, n, device):
        return pltpu.make_async_remote_copy(
            src_ref=sent.at[(*lead, n)], dst_ref=got.at[(*lead, n)],
            send_sem=ssem.at[(*lead, n)], recv_sem=rsem.at[(*lead, n)],
            device_id=device, device_id_type=MESH,
        )

    def ring_step(size, me, up, down, step, own, lead, bufs):
        sent, got, ssem, rsem = bufs
        for direction, half, steps, start in chains(size):
            if steps < step:
                continue
            device = up if direction == 1 else down
            target = lax.rem(me + direction * (steps - step + 1) + size, size)
            block = own(target, half)
            n = start + step - 1
            if step > 1:
                message(sent, got, ssem, rsem, lead, n - 1, device).wait_recv()
                block = block + decode(got[(*lead, n - 1)])
            sent[(*lead, n)] = encode(block)
            message(sent, got, ssem, rsem, lead, n, device).start()

    def ring_last(size, me, up, down, own, lead, bufs, store):
        sent, got, ssem, rsem = bufs
        for half in (FIRST, SECOND):
            block = own(me, half)
            for direction, chain_half, steps, start in chains(size):
                if chain_half is half and steps:
                    n = start + steps - 1
                    device = up if direction == 1 else down
                    message(sent, got, ssem, rsem, lead, n, device).wait_recv()
                    block = block + decode(got[(*lead, n)])
            store(half, block)

    def ring_sent(size, up, down, lead, bufs):
        sent, got, ssem, rsem = bufs
        for direction, half, steps, start in chains(size):
            for n in range(start, start + steps):
                device = up if direction == 1 else down
                message(sent, got, ssem, rsem, lead, n, device).wait_send()

    bufs_x, bufs_z = (sent_x, got_x, sx, rx), (sent_z, got_z, sz, rz)
    bufs_z2, bufs_x2 = (sent_z2, got_z2, sz2, rz2), (sent_x2, got_x2, sx2, rx2)
    ring_x, ring_z = (XS, x, x_up, x_down), (ZS, z, z_up, z_down)

    def own_x(chunk):
        return lambda d, half: partial[chunk, d, :, :, half].reshape(ZS, PAD, HD)

    def own_z(chunk):
        return lambda d, half: partial[XC + chunk, :, d, :, half].reshape(XS, PAD, HD)

    def step_x(chunk, step):
        ring_step(*ring_x, step, own_x(chunk), (chunk,), bufs_x)

    def step_z(chunk, step):
        ring_step(*ring_z, step, own_z(chunk), (chunk,), bufs_z)

    root = HD**-0.5
    wide = (((1,), (1,)), ((), ()))

    def pair(p, carry):
        cols = pl.ds(pl.multiple_of(p * PAIR, PAIR), PAIR)

        def apart(rows):
            left = lax.broadcasted_iota(jnp.int32, rows.shape, 1) < HD
            rows = rows.astype(F32)
            return jnp.concatenate(
                [jnp.where(left, rows, 0.0), jnp.where(left, 0.0, rows)], 0
            ).astype(BF16)

        for i in range(2):
            tokens = normed[i].reshape(KEYS, E)
            keys = jnp.dot(tokens, weights[0, :, cols], preferred_element_type=F32).astype(BF16)
            values = jnp.dot(tokens, weights[1, :, cols], preferred_element_type=F32).astype(BF16)
            q = apart(query_rows[i, :, cols])
            og = apart(grad_rows[i, :, cols])
            alive = live[i] > 0.0
            scores = lax.dot_general(keys, q, wide, preferred_element_type=F32) * root
            top = jnp.max(jnp.where(alive, scores, -1000000000.0), axis=0, keepdims=True)
            weighed = jnp.where(alive, jnp.exp(scores - top), 0.0)
            total = jnp.maximum(jnp.sum(weighed, axis=0, keepdims=True), 1.0)
            probs = weighed / total
            rows_at = pl.ds(i * KEYS, KEYS)
            value_grads[rows_at, :] = jnp.dot(
                probs.astype(BF16), og, preferred_element_type=F32
            ).astype(BF16)
            prob_grads = lax.dot_general(values, og, wide, preferred_element_type=F32)
            delta = jnp.sum(prob_grads * probs, axis=0, keepdims=True)
            score_grads = (probs * (prob_grads - delta) * root).astype(BF16)
            key_grads[rows_at, :] = jnp.dot(
                score_grads, q, preferred_element_type=F32
            ).astype(BF16)

        value_chunk = jnp.where(p < ZC, XC + p, XC - 1)
        partial[p] = jnp.dot(
            turned[...], key_grads[...], preferred_element_type=F32
        ).reshape(XS, ZS, PAD, PAIR)
        step_x(p, 1)
        partial[value_chunk] = jnp.dot(
            turned[...], value_grads[...], preferred_element_type=F32
        ).reshape(XS, ZS, PAD, PAIR)

        @pl.when(p < ZC)
        def _():
            step_z(p, 1)

        @pl.when(p == ZC)
        def _():
            step_x(XC - 1, 1)

        return carry

    lax.fori_loop(0, PAIRS, pair, 0)

    def each(count, work):
        lax.fori_loop(0, count, lambda c, carry: (work(c), carry)[1], 0)

    def last_x(chunk):
        def store(half, block):
            mid_z[:, chunk, :, half] = block

        ring_last(*ring_x, own_x(chunk), (chunk,), bufs_x, store)

    def last_z(chunk):
        def store(half, block):
            mid_x[:, chunk, :, half] = block

        ring_last(*ring_z, own_z(chunk), (chunk,), bufs_z, store)

    own_z2 = lambda d, half: mid_z[d, :, :, half]
    own_x2 = lambda d, half: mid_x[d, :, :, half]
    step_z2 = lambda step: ring_step(*ring_z, step, own_z2, (), bufs_z2)
    step_x2 = lambda step: ring_step(*ring_x, step, own_x2, (), bufs_x2)

    each(ZC, lambda c: step_z(c, 2))
    each(XC, lambda c: step_x(c, 2))
    each(ZC, lambda c: step_z(c, 3))
    each(XC, last_x)
    step_z2(1)
    each(ZC, lambda c: step_z(c, 4))
    each(ZC, last_z)
    step_x2(1)
    step_z2(2)
    step_x2(2)
    step_z2(3)

    def store_x2(half, block):
        for c in range(ZC):
            final[1, :, c * PAIR + half.start : c * PAIR + half.stop] = block[c]

    ring_last(*ring_x, own_x2, (), bufs_x2, store_x2)
    step_z2(4)

    def store_z2(half, block):
        for c in range(XC):
            kind, p = (0, c) if c < PAIRS else (1, PAIRS - 1)
            final[kind, :, p * PAIR + half.start : p * PAIR + half.stop] = block[c]

    ring_last(*ring_z, own_z2, (), bufs_z2, store_z2)

    give = remote(final.at[other], swapped, 11, mate)
    give.start()
    out[0, :, own_cols] = final[g, :ROWS, :]
    give.wait_recv()
    out[0, :, mate_cols] = swapped[:ROWS, :]

    for copy in (
        to_up, to_down, up_half, down_half, mate_below, mate_above, mate_far_low, mate_far_high,
        weight_swap, shift_q, shift_g, give,
    ):
        copy.wait_send()
    each(XC, lambda c: ring_sent(XS, x_up, x_down, (c,), bufs_x))
    each(ZC, lambda c: ring_sent(ZS, z_up, z_down, (c,), bufs_z))
    ring_sent(ZS, z_up, z_down, (), bufs_z2)
    ring_sent(XS, x_up, x_down, (), bufs_x2)


def per_device(neighbour_states, queries, out_grad, kv_weight, counts, token_mask):
    x_msgs, z_msgs = 2 * XS - 2, 2 * ZS - 2
    vmem, dma = pltpu.VMEM, pltpu.SemaphoreType.DMA
    in_vmem = pl.BlockSpec(memory_space=pltpu.VMEM)
    anywhere = pl.BlockSpec(memory_space=pl.ANY)
    return pl.pallas_call(
        kernel,
        out_shape=jax.ShapeDtypeStruct((1, ROWS, 2 * COLS), F32),
        in_specs=[
            pl.BlockSpec(memory_space=pltpu.SMEM), in_vmem, in_vmem, anywhere, anywhere, anywhere,
        ],
        out_specs=in_vmem,
        scratch_shapes=[
            vmem((2, SLOTS, NLEN, E), BF16),
            vmem((2, E, COLS), BF16),
            vmem((2, STRETCH, COLS), BF16),
            vmem((2, STRETCH, COLS), BF16),
            vmem((SEQ * PAD, E), BF16),
            vmem((SEQ * PAD, 2 * KEYS), BF16),
            vmem((2 * KEYS, PAIR), BF16),
            vmem((2 * KEYS, PAIR), BF16),
            vmem((2, KEYS, HD), F32),
            vmem((XC + ZC, XS, ZS, PAD, PAIR), F32),
            vmem((XC, x_msgs, ZS, PAD, HD), WIRE),
            vmem((XC, x_msgs, ZS, PAD, HD), WIRE),
            vmem((ZC, z_msgs, XS, PAD, HD), WIRE),
            vmem((ZC, z_msgs, XS, PAD, HD), WIRE),
            vmem((ZS, XC, PAD, PAIR), F32),
            vmem((XS, ZC, PAD, PAIR), F32),
            vmem((z_msgs, XC, PAD, HD), WIRE),
            vmem((z_msgs, XC, PAD, HD), WIRE),
            vmem((x_msgs, ZC, PAD, HD), WIRE),
            vmem((x_msgs, ZC, PAD, HD), WIRE),
            vmem((2, PAD, COLS), F32),
            vmem((PAD, COLS), F32),
            dma((3,)),
            dma((12,)),
            dma((12,)),
            dma((XC, x_msgs)),
            dma((XC, x_msgs)),
            dma((ZC, z_msgs)),
            dma((ZC, z_msgs)),
            dma((z_msgs,)),
            dma((z_msgs,)),
            dma((x_msgs,)),
            dma((x_msgs,)),
        ],
        compiler_params=pltpu.CompilerParams(
            collective_id=0, has_side_effects=True, vmem_limit_bytes=56 * 1024 * 1024
        ),
        cost_estimate=pl.CostEstimate(
            flops=10_000_000_000, bytes_accessed=8_000_000, transcendentals=1_000_000
        ),
    )(counts, token_mask, neighbour_states, queries, out_grad, kv_weight)


def solution(mesh):
    return jax.shard_map(
        per_device,
        mesh=mesh,
        in_specs=(
            P("seq", "tp", None, None),
            P("seq", "tp"),
            P("seq", "tp"),
            P("grp", None, "tp"),
            P(),
            P(),
        ),
        out_specs=P("grp", "seq", "tp"),
        check_vma=False,
    )
```

time: 402 us -> 102 us (0.25); the launches traced: 395 us -> 102 us
  waiting for transfers between devices: 171 us -> 0 us
  blocking collectives: 101 us -> 0 us
  Pallas kernels: 0 us -> 100 us
  matrix products: 44.1 us -> 0 us
  starting transfers between devices: 25.3 us -> 0 us
  local copies, waits for them, and re-layouts: 24 us -> 1.87 us
  other arithmetic: 14.3 us -> 0 us
  between operations: 14.2 us -> 0.01 us
    ppermute x5 -> x0, waiting for transfers between devices: 131 us -> none  [shifted_2(): return lax.ppermute(block, axis, route)]
    unnamed x1 -> x0, blocking collectives: 101 us -> none
    pallas_call x0 -> x1, Pallas kernels: none -> 100 us  [per_device(): pl.pallas_call(kernel, out_shape=jax.ShapeDtypeStruct((1, ROWS, 2 * COLS)...]
    dot_general x6 -> x0, matrix products: 44.1 us -> none  [the longest x1 17.8 us: attend_back(): jnp.einsum('chqk,cqhd->ckhd', score_grads, query_tiles, preferred_element...]
    all_gather x1 -> x0, waiting for transfers between devices: 35.2 us -> none  [per_device(): lax.all_gather(normalize(neighbour_states), 'tp', axis=1, tiled=True)]
    unnamed x4 -> x0, starting transfers between devices: 14.6 us -> none
    cond x9 -> x0, local copies, waits for them, and re-layouts: 14.2 us -> none  [the longest x2 12.6 us: per_device(): key_grads, value_grads = lax.cond(group_role == 1, decode, nothing)]
    ppermute x5 -> x0, starting transfers between devices: 10.6 us -> none  [shifted_2(): return lax.ppermute(block, axis, route)]
  transfers between devices with their start and end apart: 10 -> 0, of which waited for: 6 -> 0; matrix products, arithmetic and copies ran while one was open for 3% -> 0% of each run, Pallas kernels for 0% -> 0%
where the time goes in v1:
time: 102 us
  Pallas kernels  100 us (98%)
  local copies, waits for them, and re-layouts  1.87 us (2%)
    pallas_call x1, Pallas kernels, per_device(): pl.pallas_call(kernel, out_shape=jax.ShapeDtypeStruct((1, ROWS, 2 * COLS)...  100 us

profile of v1, /device:TPU:1, one launch (start us, length us, event | category | flops | bytes accessed | tf_op | source)
XLA Modules:
  0.0 101.9 jit_solution(7556691410099747803)
XLA Ops:
  0.0 100.0 %shard_map.64 = f32[1,28,2048]{2,1,0:T(8,128)} custom-call(s32[64]{0:T(128)} %counts.1, s32[64,4,128]{2,1,0:T(4,128)} %token_mask.1, bf16[2,1,128,896]{3,2,1,0:T(8,128)(2,1)} %states.1, bf16[128,2048]{1,0:T(8,128)(2,1)} %queries.1, bf16[128,2048]{1,0:T(8,128)(2,1)} %out_grad.1, bf16[1,896,2048]{2,1,0:T(8,128)(2,1)} %weight.1), custom_call_target="tpu_custom_call" | custom-call | flops 10000000000 | bytes 8000000 | tf_op jit(solution)/shard_map/pallas_call | solution.py:358
  100.0 1.9 %copy.7 = f32[1,28,2048]{2,0,1:T(1,128)} copy(f32[1,28,2048]{2,1,0:T(8,128)} %shard_map.64) | data formatting | bytes 458752 | tf_op jit(solution)/shard_map/pallas_call | solution.py:358

commit v2 on v0

v2 whole, which is shorter than its diff:
```python
import jax
import jax.numpy as jnp
from jax import lax
from jax.experimental import pallas as pl
from jax.experimental.pallas import tpu as pltpu
from jax.sharding import PartitionSpec as P

HD = 128
SLOTS = 4
NLEN = 128
STRETCH = 64
E = 896
ROWS = 28
PAD = 32
XS, ZS, TP = 4, 8, 4
SEQ = XS * ZS
BAND = ZS * ROWS
COLS = 1024
PAIR = 2 * HD
PAIRS = COLS // PAIR
KEYS = SLOTS * NLEN
HALF = NLEN // 2
EPS = 1e-06
POWER = 9
SPAN = 2.0**13
F32 = jnp.float32
BF16 = jnp.bfloat16
MESH = pl.DeviceIdType.MESH
FIRST, SECOND, WHOLE = slice(0, HD), slice(HD, PAIR), slice(0, PAIR)


def with_children(edges):
    found = {}

    def visit(n):
        if n not in found:
            source, _, cols = edges[n]
            under = [m for m, (_, to, other) in enumerate(edges) if to == source and other == cols]
            found[n] = (*edges[n], under, 1 + max([visit(m)[4] for m in under], default=0))
        return found[n]

    return [visit(n) for n in range(len(edges))]


def around(size):
    far = size // 2
    edges = []
    for sign, cols, steps in (
        (-1, SECOND, far), (1, FIRST, far), (-1, FIRST, far - 1), (1, SECOND, far - 1)
    ):
        edges += [(sign * k, sign * (k - 1), cols) for k in range(steps, 0, -1)]
    return with_children(edges)


def direct(size):
    far = size // 2
    return with_children([(k, 0, WHOLE) for k in range(far, -far, -1) if k])


def strides(size):
    edges = []
    for sign, cols in ((1, FIRST), (-1, SECOND)):
        edges += [(4, 2, cols), (3, 2, cols), (-3, -2, cols)] if sign == 1 else [
            (-4, -2, cols), (-3, -2, cols), (3, 2, cols)
        ]
        edges += [(k, 0, cols) for k in (2, -2, 1, -1)]
    return with_children(edges)


X_FIRST = [(0, 0), (0, 1), (0, 2), (0, 3), (1, 3)]
Z_FIRST = [(1, 0), (1, 1), (1, 2)]
X_PLANS = [around(XS), around(XS), around(XS), direct(XS), direct(XS)]
Z_PLANS = [around(ZS), around(ZS), strides(ZS)]
THEN_Z = [([0, 1], strides(ZS)), ([2, 3, 4], direct(ZS))]
THEN_X = [([0, 1, 2], direct(XS))]
PHASES = (
    [(plan, 1, BAND + 16, BAND) for plan in X_PLANS]
    + [(plan, XS, PAD, ROWS) for plan in Z_PLANS]
    + [(plan, len(group), PAD, ROWS) for group, plan in THEN_Z]
    + [(plan, len(group), PAD, ROWS) for group, plan in THEN_X]
)


def encode(block, ref, valid):
    rows = ref.shape[1]
    largest = jnp.max(jnp.abs(block), axis=1, keepdims=True)
    scale = (jnp.maximum(largest, 1e-33) * 1.01).astype(BF16).astype(F32)
    unit = block * (SPAN / scale)
    square = unit * unit
    fourth = square * square
    powers = fourth * fourth * unit
    if block.shape[1] == rows:
        row = lax.broadcasted_iota(jnp.int32, block.shape, 1)
        ref[...] = jnp.where(row < valid, powers, scale).astype(BF16)
    else:
        ref[:, :valid, :] = powers.astype(BF16)
        wide = (block.shape[0], rows - valid, block.shape[2])
        ref[:, valid:, :] = jnp.broadcast_to(scale, wide).astype(BF16)


def decode(ref, valid):
    rows = ref.shape[1]
    if rows == PAD:
        powers = ref[...].astype(F32)
        row = lax.broadcasted_iota(jnp.int32, powers.shape, 1)
        scale = jnp.where(row < valid, powers[:, valid : valid + 1, :] * (1.0 / SPAN), 0.0)
    else:
        powers = ref[:, :valid, :].astype(F32)
        scale = ref[:, valid:, :].astype(F32)[:, :1, :] * (1.0 / SPAN)
    size = jnp.exp2(jnp.log2(jnp.maximum(jnp.abs(powers), 1e-37)) * (1.0 / POWER))
    return jnp.where(powers < 0.0, -scale, scale) * size


class Reduction:
    def __init__(self, phase, refs, me, device, own, store):
        self.plan, _, _, self.valid = phase
        self.sent, self.got, self.send_sem, self.recv_sem = refs
        self.me, self.device, self.own, self.store = me, device, own, store

    def copy(self, n):
        source, target, _, _, _ = self.plan[n]
        return pltpu.make_async_remote_copy(
            src_ref=self.sent.at[n], dst_ref=self.got.at[n],
            send_sem=self.send_sem.at[n], recv_sem=self.recv_sem.at[n],
            device_id=self.device(target - source), device_id_type=MESH,
        )

    def summed(self, offset, cols, under):
        block = self.own(self.me(-offset), cols)
        for n in under:
            self.copy(n).wait_recv()
            block = block + decode(self.got.at[n], self.valid)
        return block

    def step(self, step):
        for n, (source, _, cols, under, at) in enumerate(self.plan):
            if at == step:
                encode(self.summed(source, cols, under), self.sent.at[n], self.valid)
                self.copy(n).start()

    def last(self):
        for cols in sorted({edge[2].start for edge in self.plan}):
            under = [n for n, e in enumerate(self.plan) if e[1] == 0 and e[2].start == cols]
            cols = self.plan[under[0]][2]
            self.store(cols, self.summed(0, cols, under))

    def wait_sent(self):
        for n in range(len(self.plan)):
            self.copy(n).wait_send()


def kernel(
    counts, token_mask, states, queries, out_grad, weight, out,
    count_here, mask_here, states_here, normed, weights, query_rows, grad_rows, bias,
    projected, key_grads, value_grads, part_x, part_z, final, swapped, local_sem, gs, gr, *rest,
):
    g = lax.axis_index("grp")
    s = lax.axis_index("seq")
    t = lax.axis_index("tp")
    x, z = lax.div(s, ZS), lax.rem(s, ZS)
    other = 1 - g
    along_x = lambda by: (g, lax.rem(x + by + XS, XS) * ZS + z, t)
    along_z = lambda by: (g, x * ZS + lax.rem(z + by + ZS, ZS), t)
    s_up, s_down = (g, lax.rem(s + 1, SEQ), t), (g, lax.rem(s + SEQ - 1, SEQ), t)
    y_up, y_down = (g, s, lax.rem(t + 1, TP)), (g, s, lax.rem(t + TP - 1, TP))
    mate = (other, s, t)

    barrier = pltpu.get_barrier_semaphore()
    everyone = [mate, y_up, y_down, s_up, s_down]
    everyone += [along_x(by) for by in (1, -1, 2)]
    everyone += [along_z(by) for by in (1, -1, 2, -2, 3, -3, 4)]
    for device in everyone:
        pl.semaphore_signal(barrier, inc=1, device_id=device, device_id_type=MESH)

    own_cols = pl.ds(pl.multiple_of(g * COLS, COLS), COLS)
    mate_cols = pl.ds(pl.multiple_of(other * COLS, COLS), COLS)
    top_rows, bottom_rows = pl.ds(0, STRETCH), pl.ds(STRETCH, STRETCH)
    here = [
        pltpu.make_async_copy(source, target, local_sem.at[n])
        for n, (source, target) in enumerate((
            (states.at[:, 0], states_here),
            (token_mask.at[pl.ds(2 * s, 2)], mask_here),
            (counts, count_here),
            (weight.at[0, :, own_cols], weights.at[g]),
            (queries.at[bottom_rows, own_cols], query_rows.at[0]),
            (out_grad.at[bottom_rows, own_cols], grad_rows.at[0]),
        ))
    ]
    for copy in here:
        copy.start()

    def normalize(i):
        rows = states_here[i].astype(F32)
        mean_sq = jnp.mean(rows * rows, axis=-1, keepdims=True)
        normed[i, :NLEN, :] = (rows * lax.rsqrt(mean_sq + EPS)).astype(BF16)

    here[0].wait()
    normalize(g)
    pl.semaphore_wait(barrier, len(everyone))

    def remote(src, dst, index, device):
        return pltpu.make_async_remote_copy(
            src_ref=src, dst_ref=dst, send_sem=gs.at[index], recv_sem=gr.at[index],
            device_id=device, device_id_type=MESH,
        )

    def half(core, slot, high):
        return normed.at[core, pl.ds(slot * NLEN + high * HALF, HALF)]

    started = []

    def send(source, target, index, device):
        copy = remote(source, target, index, device)
        copy.start()
        started.append(copy)

    def arrived(piece, index):
        remote(piece, piece, index, mate).wait_recv()

    send(half(g, 0, 0), half(g, 3, 0), 0, y_up)
    send(half(g, 0, 1), half(g, 1, 1), 1, y_down)
    send(half(g, 0, 1), half(g, 3, 1), 2, y_up)
    send(half(g, 0, 0), half(g, 1, 0), 3, y_down)
    send(weight.at[0, :, mate_cols], weights.at[g], 12, mate)
    send(queries.at[top_rows, own_cols], query_rows.at[1], 13, s_down)
    send(out_grad.at[top_rows, own_cols], grad_rows.at[1], 14, s_down)

    normalize(other)

    def project(rows, stores, p):
        cols = pl.ds(pl.multiple_of(p * PAIR, PAIR), PAIR)
        for kind in range(2):
            result = jnp.dot(rows, weights[kind, :, cols], preferred_element_type=F32).astype(BF16)
            for n, (i, slot) in enumerate(stores):
                at = slice(slot * NLEN, (slot + 1) * NLEN)
                projected[kind, p, i, at, :] = result[n * NLEN : (n + 1) * NLEN, :]

    def project_slots(slots, p):
        stores = [(i, slot) for i in range(2) for slot in slots]
        rows = [normed[i, slot * NLEN : (slot + 1) * NLEN, :] for i, slot in stores]
        project(jnp.concatenate(rows, 0), stores, p)

    def each(start, stop, work):
        lax.fori_loop(start, stop, lambda c, carry: (work(c), carry)[1], 0)

    here[1].wait()
    here[2].wait()
    token = lax.broadcasted_iota(jnp.int32, (NLEN, HD), 0).astype(F32)
    for i in range(2):
        c = 2 * s + i
        count = jnp.where(c == 2 * SEQ - 1, 0, count_here[c])
        for n in range(SLOTS):
            slot = lax.rem(t + n, TP)
            length = jnp.sum(mask_here[i, pl.ds(slot, 1), :].astype(F32), axis=1, keepdims=True)
            bound = length * jnp.where(slot < count, 1.0, 0.0)
            bias[i, n * NLEN : (n + 1) * NLEN, :] = jnp.where(token < bound, 0.0, -1e30)

    arrived(half(g, 3, 0), 0)
    send(half(g, 3, 0), half(g, 2, 0), 4, y_up)
    arrived(half(g, 1, 1), 1)
    send(half(g, 1, 1), half(g, 2, 1), 5, y_down)
    send(half(g, 3, 0), half(g, 3, 0), 6, mate)
    send(half(g, 1, 1), half(g, 1, 1), 7, mate)
    for copy in here[3:]:
        copy.wait()
    arrived(weights.at[other], 12)
    each(0, 2, lambda p: project_slots([0], p))
    arrived(half(g, 3, 1), 2)
    send(half(g, 3, 1), half(g, 3, 1), 8, mate)
    arrived(half(g, 1, 0), 3)
    send(half(g, 1, 0), half(g, 1, 0), 9, mate)
    each(2, PAIRS, lambda p: project_slots([0], p))
    arrived(half(other, 3, 0), 6)
    arrived(half(other, 1, 1), 7)
    arrived(half(other, 3, 1), 8)
    arrived(half(other, 1, 0), 9)
    each(0, 1, lambda p: project_slots([1, 3], p))
    arrived(half(g, 2, 0), 4)
    send(half(g, 2, 0), half(g, 2, 0), 10, mate)
    arrived(half(g, 2, 1), 5)
    send(half(g, 2, 1), half(g, 2, 1), 11, mate)
    each(1, PAIRS, lambda p: project_slots([1, 3], p))
    arrived(query_rows.at[1], 13)
    arrived(grad_rows.at[1], 14)
    arrived(half(other, 2, 0), 10)
    arrived(half(other, 2, 1), 11)

    rest = list(rest)
    mids = [rest.pop(0) for _ in THEN_Z + THEN_X]
    refs = [tuple(rest[4 * n : 4 * n + 4]) for n in range(len(PHASES))]
    me_x = lambda by: lax.rem(x + by + XS, XS)
    me_z = lambda by: lax.rem(z + by + ZS, ZS)
    place = {}
    for n, (group, _) in enumerate(THEN_Z):
        place.update({X_FIRST[c]: (mids[n], k) for k, c in enumerate(group)})
    for n, (group, _) in enumerate(THEN_X):
        place.update({Z_FIRST[c]: (mids[len(THEN_Z) + n], k) for k, c in enumerate(group)})
    for ref in (part_z, *mids):
        ref[..., PAD - 8 :, :] = jnp.zeros((*ref.shape[:-2], 8, PAIR), F32)

    def first_x(n):
        mid, k = place[X_FIRST[n]]

        def store(cols, block):
            for b in range(ZS):
                mid[b, k, :ROWS, cols] = block[0, b * ROWS : (b + 1) * ROWS, :]

        own = lambda d, cols: part_x[n, d, :, cols].reshape(1, BAND, -1)
        return Reduction(PHASES[n], refs[n], me_x, along_x, own, store)

    def first_z(n):
        mid, k = place[Z_FIRST[n]]

        def store(cols, block):
            mid[:, k, :, cols] = block

        own = lambda d, cols: part_z[n, :, d, :, cols]
        m = len(X_FIRST) + n
        return Reduction(PHASES[m], refs[m], me_z, along_z, own, store)

    def then(m, mid, group, pieces, me, device):
        def store(cols, block):
            for k, c in enumerate(group):
                kind, p = pieces[c]
                final[kind, :, p * PAIR + cols.start : p * PAIR + cols.stop] = block[k]

        own = lambda d, cols: mid[d, :, :, cols]
        return Reduction(PHASES[m], refs[m], me, device, own, store)

    xs = [first_x(n) for n in range(len(X_FIRST))]
    zs = [first_z(n) for n in range(len(Z_FIRST))]
    m = len(xs) + len(zs)
    zz = [
        then(m + n, mids[n], group, X_FIRST, me_z, along_z)
        for n, (group, _) in enumerate(THEN_Z)
    ]
    m += len(zz)
    xx = [
        then(m + n, mids[len(zz) + n], group, Z_FIRST, me_x, along_x)
        for n, (group, _) in enumerate(THEN_X)
    ]

    root = HD**-0.5
    wide = (((1,), (1,)), ((), ()))

    def apart(rows):
        left = lax.broadcasted_iota(jnp.int32, rows.shape, 1) < HD
        rows = rows.astype(F32)
        return jnp.concatenate(
            [jnp.where(left, rows, 0.0), jnp.where(left, 0.0, rows)], 0
        ).astype(BF16)

    def attend(p):
        cols = pl.ds(pl.multiple_of(p * PAIR, PAIR), PAIR)
        for i in range(2):
            q, og = apart(query_rows[i, :, cols]), apart(grad_rows[i, :, cols])
            scores = lax.dot_general(projected[0, p, i], q, wide, preferred_element_type=F32)
            prob_grads = lax.dot_general(projected[1, p, i], og, wide, preferred_element_type=F32)
            scores = scores * root + bias[i]
            top = jnp.maximum(jnp.max(scores, axis=0, keepdims=True), -1e9)
            weighed = jnp.exp(scores - top)
            share = 1.0 / jnp.maximum(jnp.sum(weighed, axis=0, keepdims=True), 1.0)
            probs = weighed * share
            at = slice(i * KEYS, (i + 1) * KEYS)
            value_grads[at, :] = jnp.dot(
                probs.astype(BF16), og, preferred_element_type=F32
            ).astype(BF16)
            delta = jnp.sum(prob_grads * probs, axis=0, keepdims=True)
            score_grads = ((probs * root) * (prob_grads - delta)).astype(BF16)
            key_grads[at, :] = jnp.dot(score_grads, q, preferred_element_type=F32).astype(BF16)

    def gradient(grads):
        tokens = normed[...].reshape(2 * KEYS, E)
        return lax.dot_general(
            tokens, grads[...], (((0,), (0,)), ((), ())), preferred_element_type=F32
        )

    def after(p):
        if p == 0:
            zs[0].step(1)
        if p == 1:
            zs[1].step(1)
            xs[0].step(2)
            zs[0].step(2)
        if p == 2:
            zs[2].step(1)
            xs[1].step(2)
            xs[0].last()
            zs[0].step(3)
            zs[1].step(2)
        if p == 3:
            xs[4].step(1)
            xs[2].step(2)
            xs[1].last()
            zz[0].step(1)
            zs[2].step(2)
            zs[0].step(4)
            zs[1].step(3)

    def pair(p, carry):
        project_slots([2], p)
        attend(p)
        part_x[p] = gradient(key_grads).reshape(XS, BAND, PAIR)
        for n in range(PAIRS):
            pl.when(p == n)(lambda n=n: xs[n].step(1))

        @pl.when(p < PAIRS - 1)
        def _():
            result = gradient(value_grads)
            for b in range(SEQ):
                part_z[p, b // ZS, b % ZS, :ROWS, :] = result[b * ROWS : (b + 1) * ROWS, :]

        @pl.when(p == PAIRS - 1)
        def _():
            part_x[PAIRS] = gradient(value_grads).reshape(XS, BAND, PAIR)

        for n in range(PAIRS):
            pl.when(p == n)(lambda n=n: after(n))
        return carry

    lax.fori_loop(0, PAIRS, pair, 0)
    xs[2].last()
    zs[1].step(4)
    zs[0].last()
    zz[0].step(2)
    zs[2].last()
    xs[3].last()
    xs[4].last()
    zz[1].step(1)
    zs[1].last()
    xx[0].step(1)
    zz[0].last()
    xx[0].last()
    zz[1].last()

    give = remote(final.at[other], swapped, 15, mate)
    give.start()
    out[0, :, own_cols] = final[g, :ROWS, :]
    give.wait_recv()
    out[0, :, mate_cols] = swapped[:ROWS, :]

    for copy in (*started, give):
        copy.wait_send()
    for reduction in (*xs, *zs, *zz, *xx):
        reduction.wait_sent()


def per_device(neighbour_states, queries, out_grad, kv_weight, counts, token_mask):
    vmem, dma = pltpu.VMEM, pltpu.SemaphoreType.DMA
    anywhere = pl.BlockSpec(memory_space=pl.ANY)
    scratch = [
        pltpu.SMEM(counts.shape, jnp.int32),
        vmem((2, SLOTS, NLEN), jnp.int32),
        vmem((2, NLEN, E), BF16),
        vmem((2, KEYS, E), BF16),
        vmem((2, E, COLS), BF16),
        vmem((2, STRETCH, COLS), BF16),
        vmem((2, STRETCH, COLS), BF16),
        vmem((2, KEYS, HD), F32),
        vmem((2, PAIRS, 2, KEYS, PAIR), BF16),
        vmem((2 * KEYS, PAIR), BF16),
        vmem((2 * KEYS, PAIR), BF16),
        vmem((len(X_FIRST), XS, BAND, PAIR), F32),
        vmem((len(Z_FIRST), XS, ZS, PAD, PAIR), F32),
        vmem((2, PAD, COLS), F32),
        vmem((PAD, COLS), F32),
        dma((6,)),
        dma((16,)),
        dma((16,)),
    ]
    scratch += [vmem((ZS, len(group), PAD, PAIR), F32) for group, _ in THEN_Z]
    scratch += [vmem((XS, len(group), PAD, PAIR), F32) for group, _ in THEN_X]
    for plan, blocks, rows, _ in PHASES:
        width = plan[0][2].stop - plan[0][2].start
        scratch += [vmem((len(plan), blocks, rows, width), BF16)] * 2
        scratch += [dma((len(plan),))] * 2
    return pl.pallas_call(
        kernel,
        out_shape=jax.ShapeDtypeStruct((1, ROWS, 2 * COLS), F32),
        in_specs=[anywhere] * 6,
        out_specs=pl.BlockSpec(memory_space=pltpu.VMEM),
        scratch_shapes=scratch,
        compiler_params=pltpu.CompilerParams(
            collective_id=0, has_side_effects=True, vmem_limit_bytes=60 * 1024 * 1024
        ),
        cost_estimate=pl.CostEstimate(
            flops=10_000_000_000, bytes_accessed=8_000_000, transcendentals=1_000_000
        ),
    )(counts, token_mask, neighbour_states, queries, out_grad, kv_weight)


def solution(mesh):
    return jax.shard_map(
        per_device,
        mesh=mesh,
        in_specs=(
            P("seq", "tp", None, None),
            P("seq", "tp"),
            P("seq", "tp"),
            P("grp", None, "tp"),
            P(),
            P(),
        ),
        out_specs=P("grp", "seq", "tp"),
        check_vma=False,
    )
```

time: 402 us -> 70.2 us (0.17); the launches traced: 395 us -> 70.1 us
  waiting for transfers between devices: 171 us -> 0 us
  blocking collectives: 101 us -> 0 us
  Pallas kernels: 0 us -> 68.2 us
  matrix products: 44.1 us -> 0 us
  starting transfers between devices: 25.3 us -> 0 us
  local copies, waits for them, and re-layouts: 24 us -> 1.87 us
  other arithmetic: 14.3 us -> 0 us
  between operations: 14.2 us -> 0.01 us
    ppermute x5 -> x0, waiting for transfers between devices: 131 us -> none  [shifted_2(): return lax.ppermute(block, axis, route)]
    unnamed x1 -> x0, blocking collectives: 101 us -> none
    pallas_call x0 -> x1, Pallas kernels: none -> 68.2 us  [per_device(): pl.pallas_call(kernel, out_shape=jax.ShapeDtypeStruct((1, ROWS, 2 * COLS)...]
    dot_general x6 -> x0, matrix products: 44.1 us -> none  [the longest x1 17.8 us: attend_back(): jnp.einsum('chqk,cqhd->ckhd', score_grads, query_tiles, preferred_element...]
    all_gather x1 -> x0, waiting for transfers between devices: 35.2 us -> none  [per_device(): lax.all_gather(normalize(neighbour_states), 'tp', axis=1, tiled=True)]
    unnamed x4 -> x0, starting transfers between devices: 14.6 us -> none
    cond x9 -> x0, local copies, waits for them, and re-layouts: 14.2 us -> none  [the longest x2 12.6 us: per_device(): key_grads, value_grads = lax.cond(group_role == 1, decode, nothing)]
    ppermute x5 -> x0, starting transfers between devices: 10.6 us -> none  [shifted_2(): return lax.ppermute(block, axis, route)]
  transfers between devices with their start and end apart: 10 -> 0, of which waited for: 6 -> 0; matrix products, arithmetic and copies ran while one was open for 3% -> 0% of each run, Pallas kernels for 0% -> 0%
where the time goes in v2:
time: 70.2 us; the launch traced here: 70.1 us
  Pallas kernels  68.2 us (97%)
  local copies, waits for them, and re-layouts  1.87 us (3%)
    pallas_call x1, Pallas kernels, per_device(): pl.pallas_call(kernel, out_shape=jax.ShapeDtypeStruct((1, ROWS, 2 * COLS)...  68.2 us
    pallas_call x1, local copies, waits for them, and re-layouts, per_device(): pl.pallas_call(kernel, out_shape=jax.ShapeDtypeStruct((1, ROWS, 2 * COLS)...  1.87 us

profile of v2, /device:TPU:1, one launch (start us, length us, event | category | flops | bytes accessed | tf_op | source)
XLA Modules:
  0.0 70.1 jit_solution(17714249244487774600)
XLA Ops:
  0.0 68.2 %shard_map.64 = f32[1,28,2048]{2,1,0:T(8,128)} custom-call(s32[64]{0:T(128)} %counts.1, s32[64,4,128]{2,1,0:T(4,128)} %token_mask.1, bf16[2,1,128,896]{3,2,1,0:T(8,128)(2,1)} %states.1, bf16[128,2048]{1,0:T(8,128)(2,1)} %queries.1, bf16[128,2048]{1,0:T(8,128)(2,1)} %out_grad.1, bf16[1,896,2048]{2,1,0:T(8,128)(2,1)} %weight.1), custom_call_target="tpu_custom_call" | custom-call | flops 10000000000 | bytes 8000000 | tf_op jit(solution)/shard_map/pallas_call | solution.py:477
  68.2 1.9 %copy.7 = f32[1,28,2048]{2,0,1:T(1,128)} copy(f32[1,28,2048]{2,1,0:T(8,128)} %shard_map.64) | data formatting | bytes 458752 | tf_op jit(solution)/shard_map/pallas_call | solution.py:477

commit v3 on v2

--- a/solution.py
+++ b/solution.py
@@ -67,15 +67,23 @@
     return with_children(edges)
 
 
-X_FIRST = [(0, 0), (0, 1), (0, 2), (0, 3), (1, 3)]
-Z_FIRST = [(1, 0), (1, 1), (1, 2)]
-X_PLANS = [around(XS), around(XS), around(XS), direct(XS), direct(XS)]
-Z_PLANS = [around(ZS), around(ZS), strides(ZS)]
-THEN_Z = [([0, 1], strides(ZS)), ([2, 3, 4], direct(ZS))]
-THEN_X = [([0, 1, 2], direct(XS))]
+X_FIRST = [((1, 1), around(XS)), ((1, 2), around(XS)), ((0, 3), around(XS)), ((1, 3), around(XS))]
+Z_FIRST = [((0, 0), around(ZS)), ((1, 0), around(ZS)), ((0, 1), around(ZS)), ((0, 2), around(ZS))]
+THEN_Z = [([0], around(ZS)), ([1], strides(ZS)), ([2], strides(ZS)), ([3], direct(ZS))]
+THEN_X = [([0, 1], around(XS)), ([2], direct(XS)), ([3], direct(XS))]
+SCHEDULE = [
+    [],
+    [(4, 1), (5, 1)],
+    [],
+    [(6, 1), (0, 1)],
+    [(4, 2), (5, 2)],
+    [(7, 1), (1, 1), (6, 2), (0, 2)],
+    [(4, 3)],
+    [(5, 3), (2, 1), (3, 1), (7, 2), (1, 2), (6, 3), (4, 4), (0, 0), (8, 1), (5, 4), (2, 2), (7, 3), (6, 4), (3, 2), (8, 2), (4, 0), (5, 0), (12, 1), (7, 4), (1, 0), (9, 1), (2, 0), (8, 3), (10, 1), (6, 0), (12, 2), (13, 1), (3, 0), (11, 1), (7, 0), (14, 1), (8, 4), (9, 2), (12, 0), (10, 2), (13, 0), (14, 0), (8, 0), (11, 0), (9, 0), (10, 0)],
+]
 PHASES = (
-    [(plan, 1, BAND + 16, BAND) for plan in X_PLANS]
-    + [(plan, XS, PAD, ROWS) for plan in Z_PLANS]
+    [(plan, 1, BAND + 16, BAND) for _, plan in X_FIRST]
+    + [(plan, XS, PAD, ROWS) for _, plan in Z_FIRST]
     + [(plan, len(group), PAD, ROWS) for group, plan in THEN_Z]
     + [(plan, len(group), PAD, ROWS) for group, plan in THEN_X]
 )
@@ -152,7 +160,7 @@
 def kernel(
     counts, token_mask, states, queries, out_grad, weight, out,
     count_here, mask_here, states_here, normed, weights, query_rows, grad_rows, bias,
-    projected, key_grads, value_grads, part_x, part_z, final, swapped, local_sem, gs, gr, *rest,
+    projected, grads, part, part_z, final, swapped, local_sem, gs, gr, *rest,
 ):
     g = lax.axis_index("grp")
     s = lax.axis_index("seq")
@@ -292,24 +300,28 @@
     me_z = lambda by: lax.rem(z + by + ZS, ZS)
     place = {}
     for n, (group, _) in enumerate(THEN_Z):
-        place.update({X_FIRST[c]: (mids[n], k) for k, c in enumerate(group)})
+        place.update({X_FIRST[c][0]: (mids[n], k) for k, c in enumerate(group)})
     for n, (group, _) in enumerate(THEN_X):
-        place.update({Z_FIRST[c]: (mids[len(THEN_Z) + n], k) for k, c in enumerate(group)})
+        place.update({Z_FIRST[c][0]: (mids[len(THEN_Z) + n], k) for k, c in enumerate(group)})
     for ref in (part_z, *mids):
         ref[..., PAD - 8 :, :] = jnp.zeros((*ref.shape[:-2], 8, PAIR), F32)
 
     def first_x(n):
-        mid, k = place[X_FIRST[n]]
+        kind, p = X_FIRST[n][0]
+        mid, k = place[kind, p]
 
         def store(cols, block):
             for b in range(ZS):
                 mid[b, k, :ROWS, cols] = block[0, b * ROWS : (b + 1) * ROWS, :]
 
-        own = lambda d, cols: part_x[n, d, :, cols].reshape(1, BAND, -1)
+        def own(d, cols):
+            at = slice(kind * PAIR + cols.start, kind * PAIR + cols.stop)
+            return part[p, pl.ds(d, 1), :, at]
+
         return Reduction(PHASES[n], refs[n], me_x, along_x, own, store)
 
     def first_z(n):
-        mid, k = place[Z_FIRST[n]]
+        mid, k = place[Z_FIRST[n][0]]
 
         def store(cols, block):
             mid[:, k, :, cols] = block
@@ -321,7 +333,7 @@
     def then(m, mid, group, pieces, me, device):
         def store(cols, block):
             for k, c in enumerate(group):
-                kind, p = pieces[c]
+                kind, p = pieces[c][0]
                 final[kind, :, p * PAIR + cols.start : p * PAIR + cols.stop] = block[k]
 
         own = lambda d, cols: mid[d, :, :, cols]
@@ -352,86 +364,73 @@
 
     def attend(p):
         cols = pl.ds(pl.multiple_of(p * PAIR, PAIR), PAIR)
-        for i in range(2):
-            q, og = apart(query_rows[i, :, cols]), apart(grad_rows[i, :, cols])
-            scores = lax.dot_general(projected[0, p, i], q, wide, preferred_element_type=F32)
-            prob_grads = lax.dot_general(projected[1, p, i], og, wide, preferred_element_type=F32)
-            scores = scores * root + bias[i]
+        both = range(2)
+        q = [apart(query_rows[i, :, cols]) for i in both]
+        og = [apart(grad_rows[i, :, cols]) for i in both]
+        score = [
+            lax.dot_general(projected[0, p, i], q[i], wide, preferred_element_type=F32) for i in both
+        ]
+        prob_grad = [
+            lax.dot_general(projected[1, p, i], og[i], wide, preferred_element_type=F32) for i in both
+        ]
+        for i in both:
+            scores = score[i] * root + bias[i]
             top = jnp.maximum(jnp.max(scores, axis=0, keepdims=True), -1e9)
             weighed = jnp.exp(scores - top)
             share = 1.0 / jnp.maximum(jnp.sum(weighed, axis=0, keepdims=True), 1.0)
             probs = weighed * share
+            delta = jnp.sum(prob_grad[i] * probs, axis=0, keepdims=True)
+            score_grads = ((probs * root) * (prob_grad[i] - delta)).astype(BF16)
             at = slice(i * KEYS, (i + 1) * KEYS)
-            value_grads[at, :] = jnp.dot(
-                probs.astype(BF16), og, preferred_element_type=F32
+            grads[at, PAIR:] = jnp.dot(
+                probs.astype(BF16), og[i], preferred_element_type=F32
             ).astype(BF16)
-            delta = jnp.sum(prob_grads * probs, axis=0, keepdims=True)
-            score_grads = ((probs * root) * (prob_grads - delta)).astype(BF16)
-            key_grads[at, :] = jnp.dot(score_grads, q, preferred_element_type=F32).astype(BF16)
-
-    def gradient(grads):
-        tokens = normed[...].reshape(2 * KEYS, E)
-        return lax.dot_general(
-            tokens, grads[...], (((0,), (0,)), ((), ())), preferred_element_type=F32
-        )
-
-    def after(p):
-        if p == 0:
-            zs[0].step(1)
-        if p == 1:
-            zs[1].step(1)
-            xs[0].step(2)
-            zs[0].step(2)
-        if p == 2:
-            zs[2].step(1)
-            xs[1].step(2)
-            xs[0].last()
-            zs[0].step(3)
-            zs[1].step(2)
-        if p == 3:
-            xs[4].step(1)
-            xs[2].step(2)
-            xs[1].last()
-            zz[0].step(1)
-            zs[2].step(2)
-            zs[0].step(4)
-            zs[1].step(3)
+            grads[at, :PAIR] = jnp.dot(score_grads, q[i], preferred_element_type=F32).astype(BF16)
+
+    reductions = [*xs, *zs, *zz, *xx]
+
+    def advance(actions):
+        for n, step in actions:
+            if step:
+                reductions[n].step(step)
+            else:
+                reductions[n].last()
+
+    def pad(n):
+        kind, p = Z_FIRST[n][0]
+        at = slice(kind * PAIR, (kind + 1) * PAIR)
+        for b in range(SEQ):
+            row = b % ZS * ROWS
+            part_z[n, b // ZS, b % ZS, :ROWS, :] = part[p, b // ZS, row : row + ROWS, at]
+
+    def after(p, actions):
+        for n, (piece, _) in enumerate(Z_FIRST):
+            if piece[1] == p:
+                pad(n)
+        advance(actions)
 
     def pair(p, carry):
         project_slots([2], p)
         attend(p)
-        part_x[p] = gradient(key_grads).reshape(XS, BAND, PAIR)
         for n in range(PAIRS):
-            pl.when(p == n)(lambda n=n: xs[n].step(1))
-
-        @pl.when(p < PAIRS - 1)
-        def _():
-            result = gradient(value_grads)
-            for b in range(SEQ):
-                part_z[p, b // ZS, b % ZS, :ROWS, :] = result[b * ROWS : (b + 1) * ROWS, :]
-
-        @pl.when(p == PAIRS - 1)
-        def _():
-            part_x[PAIRS] = gradient(value_grads).reshape(XS, BAND, PAIR)
-
-        for n in range(PAIRS):
-            pl.when(p == n)(lambda n=n: after(n))
+            if SCHEDULE[2 * n]:
+                pl.when(p == n)(lambda n=n: advance(SCHEDULE[2 * n]))
+        part[p] = lax.dot_general(
+            normed[...].reshape(2 * KEYS, E), grads[...], (((0,), (0,)), ((), ())),
+            preferred_element_type=F32,
+        ).reshape(XS, BAND, 2 * PAIR)
+        for n in range(PAIRS - 1):
+            pl.when(p == n)(lambda n=n: after(n, SCHEDULE[2 * n + 1]))
         return carry
 
     lax.fori_loop(0, PAIRS, pair, 0)
-    xs[2].last()
-    zs[1].step(4)
-    zs[0].last()
-    zz[0].step(2)
-    zs[2].last()
-    xs[3].last()
-    xs[4].last()
-    zz[1].step(1)
-    zs[1].last()
-    xx[0].step(1)
-    zz[0].last()
-    xx[0].last()
-    zz[1].last()
+    late = 6
+    after(PAIRS - 1, SCHEDULE[-1][:-late])
+    for copy in started:
+        copy.wait_send()
+    for reduction in (*xs, *zs):
+        reduction.wait_sent()
+    advance(SCHEDULE[-1][-late:])
 
     give = remote(final.at[other], swapped, 15, mate)
     give.start()
@@ -439,15 +438,14 @@
     give.wait_recv()
     out[0, :, mate_cols] = swapped[:ROWS, :]
 
-    for copy in (*started, give):
-        copy.wait_send()
-    for reduction in (*xs, *zs, *zz, *xx):
+    give.wait_send()
+    for reduction in (*zz, *xx):
         reduction.wait_sent()
 
 
 def per_device(neighbour_states, queries, out_grad, kv_weight, counts, token_mask):
     vmem, dma = pltpu.VMEM, pltpu.SemaphoreType.DMA
-    anywhere = pl.BlockSpec(memory_space=pl.ANY)
+    in_hbm = pl.BlockSpec(memory_space=pltpu.HBM)
     scratch = [
         pltpu.SMEM(counts.shape, jnp.int32),
         vmem((2, SLOTS, NLEN), jnp.int32),
@@ -458,9 +456,8 @@
         vmem((2, STRETCH, COLS), BF16),
         vmem((2, KEYS, HD), F32),
         vmem((2, PAIRS, 2, KEYS, PAIR), BF16),
-        vmem((2 * KEYS, PAIR), BF16),
-        vmem((2 * KEYS, PAIR), BF16),
-        vmem((len(X_FIRST), XS, BAND, PAIR), F32),
+        vmem((2 * KEYS, 2 * PAIR), BF16),
+        vmem((PAIRS, XS, BAND, 2 * PAIR), F32),
         vmem((len(Z_FIRST), XS, ZS, PAD, PAIR), F32),
         vmem((2, PAD, COLS), F32),
         vmem((PAD, COLS), F32),
@@ -477,11 +474,11 @@
     return pl.pallas_call(
         kernel,
         out_shape=jax.ShapeDtypeStruct((1, ROWS, 2 * COLS), F32),
-        in_specs=[anywhere] * 6,
+        in_specs=[in_hbm] * 6,
         out_specs=pl.BlockSpec(memory_space=pltpu.VMEM),
         scratch_shapes=scratch,
         compiler_params=pltpu.CompilerParams(
-            collective_id=0, has_side_effects=True, vmem_limit_bytes=60 * 1024 * 1024
+            collective_id=0, has_side_effects=True, vmem_limit_bytes=56 * 1024 * 1024
         ),
         cost_estimate=pl.CostEstimate(
             flops=10_000_000_000, bytes_accessed=8_000_000, transcendentals=1_000_000

time: 70.2 us -> 63.9 us (0.910)
  Pallas kernels: 68.2 us -> 61.9 us
    pallas_call x1, Pallas kernels: 68.2 us -> 61.9 us  [per_device(): pl.pallas_call(kernel, out_shape=jax.ShapeDtypeStruct((1, ROWS, 2 * COLS)...]
where the time goes in v3:
time: 63.9 us; the launch traced here: 63.7 us
  Pallas kernels  61.9 us (97%)
  local copies, waits for them, and re-layouts  1.87 us (3%)
    pallas_call x1, Pallas kernels, per_device(): pl.pallas_call(kernel, out_shape=jax.ShapeDtypeStruct((1, ROWS, 2 * COLS)...  61.9 us
    pallas_call x1, local copies, waits for them, and re-layouts, per_device(): pl.pallas_call(kernel, out_shape=jax.ShapeDtypeStruct((1, ROWS, 2 * COLS)...  1.87 us

profile of v3, /device:TPU:1, one launch (start us, length us, event | category | flops | bytes accessed | tf_op | source)
XLA Modules:
  0.0 63.7 jit_solution(3128798314652520486)
XLA Ops:
  0.0 61.9 %shard_map.64 = f32[1,28,2048]{2,1,0:T(8,128)} custom-call(s32[64]{0:T(128)} %counts.1, s32[64,4,128]{2,1,0:T(4,128)} %token_mask.1, bf16[2,1,128,896]{3,2,1,0:T(8,128)(2,1)} %states.1, bf16[128,2048]{1,0:T(8,128)(2,1)} %queries.1, bf16[128,2048]{1,0:T(8,128)(2,1)} %out_grad.1, bf16[1,896,2048]{2,1,0:T(8,128)(2,1)} %weight.1), custom_call_target="tpu_custom_call" | custom-call | flops 10000000000 | bytes 8000000 | tf_op jit(solution)/shard_map/pallas_call | solution.py:474
  61.9 1.9 %copy.7 = f32[1,28,2048]{2,0,1:T(1,128)} copy(f32[1,28,2048]{2,1,0:T(8,128)} %shard_map.64) | data formatting | bytes 458752 | tf_op jit(solution)/shard_map/pallas_call | solution.py:474

commit v4 on v3

--- a/solution.py
+++ b/solution.py
@@ -67,19 +67,19 @@
     return with_children(edges)
 
 
-X_FIRST = [((1, 1), around(XS)), ((1, 2), around(XS)), ((0, 3), around(XS)), ((1, 3), around(XS))]
-Z_FIRST = [((0, 0), around(ZS)), ((1, 0), around(ZS)), ((0, 1), around(ZS)), ((0, 2), around(ZS))]
+X_FIRST = [((0, 1), around(XS)), ((0, 2), around(XS)), ((0, 3), around(XS)), ((1, 3), around(XS))]
+Z_FIRST = [((0, 0), around(ZS)), ((1, 0), around(ZS)), ((1, 1), around(ZS)), ((1, 2), around(ZS))]
 THEN_Z = [([0], around(ZS)), ([1], strides(ZS)), ([2], strides(ZS)), ([3], direct(ZS))]
-THEN_X = [([0, 1], around(XS)), ([2], direct(XS)), ([3], direct(XS))]
+THEN_X = [([0], direct(XS)), ([1], direct(XS)), ([2], direct(XS)), ([3], direct(XS))]
 SCHEDULE = [
     [],
     [(4, 1), (5, 1)],
     [],
-    [(6, 1), (0, 1)],
+    [(0, 1), (6, 1)],
     [(4, 2), (5, 2)],
-    [(7, 1), (1, 1), (6, 2), (0, 2)],
+    [(1, 1), (7, 1), (0, 2), (6, 2)],
     [(4, 3)],
-    [(5, 3), (2, 1), (3, 1), (7, 2), (1, 2), (6, 3), (4, 4), (0, 0), (8, 1), (5, 4), (2, 2), (7, 3), (6, 4), (3, 2), (8, 2), (4, 0), (5, 0), (12, 1), (7, 4), (1, 0), (9, 1), (2, 0), (8, 3), (10, 1), (6, 0), (12, 2), (13, 1), (3, 0), (11, 1), (7, 0), (14, 1), (8, 4), (9, 2), (12, 0), (10, 2), (13, 0), (14, 0), (8, 0), (11, 0), (9, 0), (10, 0)],
+    [(5, 3), (2, 1), (3, 1), (1, 2), (7, 2), (6, 3), (4, 4), (0, 0), (8, 1), (5, 4), (2, 2), (7, 3), (6, 4), (3, 2), (4, 0), (8, 2), (12, 1), (5, 0), (13, 1), (1, 0), (7, 4), (9, 1), (2, 0), (10, 1), (8, 3), (6, 0), (14, 1), (3, 0), (11, 1), (12, 0), (13, 0), (7, 0), (15, 1), (9, 2), (8, 4), (10, 2), (14, 0), (15, 0), (8, 0), (9, 0), (11, 0), (10, 0)],
 ]
 PHASES = (
     [(plan, 1, BAND + 16, BAND) for _, plan in X_FIRST]
@@ -121,7 +121,7 @@
 
 class Reduction:
     def __init__(self, phase, refs, me, device, own, store):
-        self.plan, _, _, self.valid = phase
+        self.plan, self.valid = phase[0], phase[3]
         self.sent, self.got, self.send_sem, self.recv_sem = refs
         self.me, self.device, self.own, self.store = me, device, own, store
 
@@ -157,10 +157,77 @@
             self.copy(n).wait_send()
 
 
+class Ending(Reduction):
+    def __init__(self, phase, refs, me, device, own, store, core, kind, mate):
+        super().__init__(phase, refs, me, device, own, store)
+        self.core, self.kind, self.mate = core, kind, mate
+        self.widths = sorted({(edge[2].start, edge[2].stop) for edge in self.plan})
+
+    def copy(self, n, source=None):
+        source = self.core if source is None else source
+        if n < len(self.plan):
+            start, end = self.plan[n][:2]
+            device = self.device(end - start)
+            if end == 0:
+                device = (self.kind, *device[1:])
+        else:
+            device = self.mate
+        return pltpu.make_async_remote_copy(
+            src_ref=self.sent.at[n], dst_ref=self.got.at[source, n],
+            send_sem=self.send_sem.at[n], recv_sem=self.recv_sem.at[source, n],
+            device_id=device, device_id_type=MESH,
+        )
+
+    def arrived(self, n, source):
+        self.copy(n, source).wait_recv()
+        return decode(self.got.at[source, n], self.valid)
+
+    def summed(self, offset, cols, under):
+        block = self.own(self.me(-offset), cols)
+        for n in under:
+            block = block + self.arrived(n, self.core)
+        return block
+
+    def step(self, step):
+        if step == 1:
+
+            @pl.when(self.core != self.kind)
+            def _():
+                for k, (start, stop) in enumerate(self.widths):
+                    n = len(self.plan) + k
+                    own = self.own(self.me(0), slice(start, stop))
+                    encode(own, self.sent.at[n], self.valid)
+                    self.copy(n).start()
+
+        super().step(step)
+
+    def last(self):
+        @pl.when(self.core == self.kind)
+        def _():
+            for source in (self.kind, 1 - self.kind):
+                for k, (start, stop) in enumerate(self.widths):
+                    if source == self.kind:
+                        block = self.own(self.me(0), slice(start, stop))
+                    else:
+                        block = self.arrived(len(self.plan) + k, source)
+                    for n, (_, end, cols, _, _) in enumerate(self.plan):
+                        if end == 0 and cols.start == start:
+                            block = block + self.arrived(n, source)
+                    self.store(source, slice(start, stop), block)
+
+    def wait_sent(self):
+        super().wait_sent()
+
+        @pl.when(self.core != self.kind)
+        def _():
+            for k in range(len(self.widths)):
+                self.copy(len(self.plan) + k).wait_send()
+
+
 def kernel(
     counts, token_mask, states, queries, out_grad, weight, out,
     count_here, mask_here, states_here, normed, weights, query_rows, grad_rows, bias,
-    projected, grads, part, part_z, final, swapped, local_sem, gs, gr, *rest,
+    projected, grads, part, part_z, local_sem, gs, gr, *rest,
 ):
     g = lax.axis_index("grp")
     s = lax.axis_index("seq")
@@ -177,6 +244,7 @@
     everyone = [mate, y_up, y_down, s_up, s_down]
     everyone += [along_x(by) for by in (1, -1, 2)]
     everyone += [along_z(by) for by in (1, -1, 2, -2, 3, -3, 4)]
+    everyone += [(other, *device[1:]) for device in everyone[5:]]
     for device in everyone:
         pl.semaphore_signal(barrier, inc=1, device_id=device, device_id_type=MESH)
 
@@ -282,12 +350,12 @@
     arrived(half(other, 1, 1), 7)
     arrived(half(other, 3, 1), 8)
     arrived(half(other, 1, 0), 9)
-    each(0, 1, lambda p: project_slots([1, 3], p))
+    each(0, 2, lambda p: project_slots([1, 3], p))
     arrived(half(g, 2, 0), 4)
     send(half(g, 2, 0), half(g, 2, 0), 10, mate)
     arrived(half(g, 2, 1), 5)
     send(half(g, 2, 1), half(g, 2, 1), 11, mate)
-    each(1, PAIRS, lambda p: project_slots([1, 3], p))
+    each(2, PAIRS, lambda p: project_slots([1, 3], p))
     arrived(query_rows.at[1], 13)
     arrived(grad_rows.at[1], 14)
     arrived(half(other, 2, 0), 10)
@@ -331,13 +399,15 @@
         return Reduction(PHASES[m], refs[m], me_z, along_z, own, store)
 
     def then(m, mid, group, pieces, me, device):
-        def store(cols, block):
+        kind = pieces[group[0]][0][0]
+
+        def store(source, cols, block):
             for k, c in enumerate(group):
-                kind, p = pieces[c][0]
-                final[kind, :, p * PAIR + cols.start : p * PAIR + cols.stop] = block[k]
+                at = source * COLS + pieces[c][0][1] * PAIR
+                out[0, :, at + cols.start : at + cols.stop] = block[k, :ROWS]
 
         own = lambda d, cols: mid[d, :, :, cols]
-        return Reduction(PHASES[m], refs[m], me, device, own, store)
+        return Ending(PHASES[m], refs[m], me, device, own, store, g, kind, mate)
 
     xs = [first_x(n) for n in range(len(X_FIRST))]
     zs = [first_z(n) for n in range(len(Z_FIRST))]
@@ -432,13 +502,6 @@
         reduction.wait_sent()
     advance(SCHEDULE[-1][-late:])
 
-    give = remote(final.at[other], swapped, 15, mate)
-    give.start()
-    out[0, :, own_cols] = final[g, :ROWS, :]
-    give.wait_recv()
-    out[0, :, mate_cols] = swapped[:ROWS, :]
-
-    give.wait_send()
     for reduction in (*zz, *xx):
         reduction.wait_sent()
 
@@ -459,18 +522,21 @@
         vmem((2 * KEYS, 2 * PAIR), BF16),
         vmem((PAIRS, XS, BAND, 2 * PAIR), F32),
         vmem((len(Z_FIRST), XS, ZS, PAD, PAIR), F32),
-        vmem((2, PAD, COLS), F32),
-        vmem((PAD, COLS), F32),
         dma((6,)),
-        dma((16,)),
-        dma((16,)),
+        dma((15,)),
+        dma((15,)),
     ]
     scratch += [vmem((ZS, len(group), PAD, PAIR), F32) for group, _ in THEN_Z]
     scratch += [vmem((XS, len(group), PAD, PAIR), F32) for group, _ in THEN_X]
-    for plan, blocks, rows, _ in PHASES:
+    for n, (plan, blocks, rows, _) in enumerate(PHASES):
         width = plan[0][2].stop - plan[0][2].start
-        scratch += [vmem((len(plan), blocks, rows, width), BF16)] * 2
-        scratch += [dma((len(plan),))] * 2
+        if n < len(X_FIRST) + len(Z_FIRST):
+            sends, receives = (len(plan),), (len(plan),)
+        else:
+            sends = (len(plan) + PAIR // width,)
+            receives = (2, *sends)
+        scratch += [vmem((*lead, blocks, rows, width), BF16) for lead in (sends, receives)]
+        scratch += [dma(sends), dma(receives)]
     return pl.pallas_call(
         kernel,
         out_shape=jax.ShapeDtypeStruct((1, ROWS, 2 * COLS), F32),

time: 63.9 us -> 61.9 us (0.969)
  Pallas kernels: 61.9 us -> 59.6 us
    pallas_call x1, Pallas kernels: 61.9 us -> 59.6 us  [per_device(): pl.pallas_call(kernel, out_shape=jax.ShapeDtypeStruct((1, ROWS, 2 * COLS)...]
where the time goes in v4:
time: 61.9 us; the launch traced here: 61.4 us
  Pallas kernels  59.6 us (96%)
  local copies, waits for them, and re-layouts  1.87 us (3%)
    pallas_call x1, Pallas kernels, per_device(): pl.pallas_call(kernel, out_shape=jax.ShapeDtypeStruct((1, ROWS, 2 * COLS)...  59.6 us
    pallas_call x1, local copies, waits for them, and re-layouts, per_device(): pl.pallas_call(kernel, out_shape=jax.ShapeDtypeStruct((1, ROWS, 2 * COLS)...  1.87 us

profile of v4, /device:TPU:1, one launch (start us, length us, event | category | flops | bytes accessed | tf_op | source)
XLA Modules:
  0.0 61.4 jit_solution(15120082675266366019)
XLA Ops:
  0.0 59.6 %shard_map.64 = f32[1,28,2048]{2,1,0:T(8,128)} custom-call(s32[64]{0:T(128)} %counts.1, s32[64,4,128]{2,1,0:T(4,128)} %token_mask.1, bf16[2,1,128,896]{3,2,1,0:T(8,128)(2,1)} %states.1, bf16[128,2048]{1,0:T(8,128)(2,1)} %queries.1, bf16[128,2048]{1,0:T(8,128)(2,1)} %out_grad.1, bf16[1,896,2048]{2,1,0:T(8,128)(2,1)} %weight.1), custom_call_target="tpu_custom_call" | custom-call | flops 10000000000 | bytes 8000000 | tf_op jit(solution)/shard_map/pallas_call | solution.py:540
  59.6 1.9 %copy.7 = f32[1,28,2048]{2,0,1:T(1,128)} copy(f32[1,28,2048]{2,1,0:T(8,128)} %shard_map.64) | data formatting | bytes 458752 | tf_op jit(solution)/shard_map/pallas_call | solution.py:540

commit v5 on v4

--- a/solution.py
+++ b/solution.py
@@ -19,7 +19,8 @@
 PAIR = 2 * HD
 PAIRS = COLS // PAIR
 KEYS = SLOTS * NLEN
-HALF = NLEN // 2
+PIECES = 4
+PIECE = NLEN // PIECES
 EPS = 1e-06
 POWER = 9
 SPAN = 2.0**13
@@ -280,8 +281,8 @@
             device_id=device, device_id_type=MESH,
         )
 
-    def half(core, slot, high):
-        return normed.at[core, pl.ds(slot * NLEN + high * HALF, HALF)]
+    def piece(core, slot, n):
+        return normed.at[core, pl.ds(slot * NLEN + n * PIECE, PIECE)]
 
     started = []
 
@@ -293,13 +294,16 @@
     def arrived(piece, index):
         remote(piece, piece, index, mate).wait_recv()
 
-    send(half(g, 0, 0), half(g, 3, 0), 0, y_up)
-    send(half(g, 0, 1), half(g, 1, 1), 1, y_down)
-    send(half(g, 0, 1), half(g, 3, 1), 2, y_up)
-    send(half(g, 0, 0), half(g, 1, 0), 3, y_down)
-    send(weight.at[0, :, mate_cols], weights.at[g], 12, mate)
-    send(queries.at[top_rows, own_cols], query_rows.at[1], 13, s_down)
-    send(out_grad.at[top_rows, own_cols], grad_rows.at[1], 14, s_down)
+    up_order = list(range(PIECES))
+    down_order = up_order[PIECES // 2 :] + up_order[: PIECES // 2]
+    lower, upper = up_order[: PIECES // 2], up_order[PIECES // 2 :]
+    UP, DOWN, FAR, MATE = 0, PIECES, 2 * PIECES, 3 * PIECES
+    for n, m in zip(up_order, down_order):
+        send(piece(g, 0, n), piece(g, 3, n), UP + n, y_up)
+        send(piece(g, 0, m), piece(g, 1, m), DOWN + m, y_down)
+    send(weight.at[0, :, mate_cols], weights.at[g], 6 * PIECES, mate)
+    send(queries.at[top_rows, own_cols], query_rows.at[1], 6 * PIECES + 1, s_down)
+    send(out_grad.at[top_rows, own_cols], grad_rows.at[1], 6 * PIECES + 2, s_down)
 
     normalize(other)
 
@@ -331,35 +335,43 @@
             bound = length * jnp.where(slot < count, 1.0, 0.0)
             bias[i, n * NLEN : (n + 1) * NLEN, :] = jnp.where(token < bound, 0.0, -1e30)
 
-    arrived(half(g, 3, 0), 0)
-    send(half(g, 3, 0), half(g, 2, 0), 4, y_up)
-    arrived(half(g, 1, 1), 1)
-    send(half(g, 1, 1), half(g, 2, 1), 5, y_down)
-    send(half(g, 3, 0), half(g, 3, 0), 6, mate)
-    send(half(g, 1, 1), half(g, 1, 1), 7, mate)
+    def pass_on(slot, n):
+        index = MATE + (slot - 1) * PIECES + n
+        send(piece(g, slot, n), piece(g, slot, n), index, mate)
+
+    def passed(slots):
+        for slot in slots:
+            for n in range(PIECES):
+                arrived(piece(other, slot, n), MATE + (slot - 1) * PIECES + n)
+
+    for n, m in zip(lower, upper):
+        arrived(piece(g, 3, n), UP + n)
+        send(piece(g, 3, n), piece(g, 2, n), FAR + n, y_up)
+        arrived(piece(g, 1, m), DOWN + m)
+        send(piece(g, 1, m), piece(g, 2, m), FAR + m, y_down)
+        pass_on(3, n)
+        pass_on(1, m)
     for copy in here[3:]:
         copy.wait()
-    arrived(weights.at[other], 12)
+    arrived(weights.at[other], 6 * PIECES)
     each(0, 2, lambda p: project_slots([0], p))
-    arrived(half(g, 3, 1), 2)
-    send(half(g, 3, 1), half(g, 3, 1), 8, mate)
-    arrived(half(g, 1, 0), 3)
-    send(half(g, 1, 0), half(g, 1, 0), 9, mate)
+    for n, m in zip(upper, lower):
+        arrived(piece(g, 3, n), UP + n)
+        pass_on(3, n)
+        arrived(piece(g, 1, m), DOWN + m)
+        pass_on(1, m)
     each(2, PAIRS, lambda p: project_slots([0], p))
-    arrived(half(other, 3, 0), 6)
-    arrived(half(other, 1, 1), 7)
-    arrived(half(other, 3, 1), 8)
-    arrived(half(other, 1, 0), 9)
-    each(0, 2, lambda p: project_slots([1, 3], p))
-    arrived(half(g, 2, 0), 4)
-    send(half(g, 2, 0), half(g, 2, 0), 10, mate)
-    arrived(half(g, 2, 1), 5)
-    send(half(g, 2, 1), half(g, 2, 1), 11, mate)
-    each(2, PAIRS, lambda p: project_slots([1, 3], p))
-    arrived(query_rows.at[1], 13)
-    arrived(grad_rows.at[1], 14)
-    arrived(half(other, 2, 0), 10)
-    arrived(half(other, 2, 1), 11)
+    passed([3, 1])
+    each(0, 1, lambda p: project_slots([1, 3], p))
+    for n, m in zip(lower, upper):
+        arrived(piece(g, 2, n), FAR + n)
+        pass_on(2, n)
+        arrived(piece(g, 2, m), FAR + m)
+        pass_on(2, m)
+    each(1, PAIRS, lambda p: project_slots([1, 3], p))
+    arrived(query_rows.at[1], 6 * PIECES + 1)
+    arrived(grad_rows.at[1], 6 * PIECES + 2)
+    passed([2])
 
     rest = list(rest)
     mids = [rest.pop(0) for _ in THEN_Z + THEN_X]
@@ -523,8 +535,8 @@
         vmem((PAIRS, XS, BAND, 2 * PAIR), F32),
         vmem((len(Z_FIRST), XS, ZS, PAD, PAIR), F32),
         dma((6,)),
-        dma((15,)),
-        dma((15,)),
+        dma((6 * PIECES + 3,)),
+        dma((6 * PIECES + 3,)),
     ]
     scratch += [vmem((ZS, len(group), PAD, PAIR), F32) for group, _ in THEN_Z]
     scratch += [vmem((XS, len(group), PAD, PAIR), F32) for group, _ in THEN_X]

time: 61.9 us -> 62.3 us (level)
  no operation moved by 1% of the time
where the time goes in v5:
time: 62.3 us; the launch traced here: 61.6 us
  Pallas kernels  59.7 us (96%)
  local copies, waits for them, and re-layouts  1.87 us (3%)
    pallas_call x1, Pallas kernels, per_device(): pl.pallas_call(kernel, out_shape=jax.ShapeDtypeStruct((1, ROWS, 2 * COLS)...  59.7 us
    pallas_call x1, local copies, waits for them, and re-layouts, per_device(): pl.pallas_call(kernel, out_shape=jax.ShapeDtypeStruct((1, ROWS, 2 * COLS)...  1.87 us

profile of v5, /device:TPU:1, one launch (start us, length us, event | category | flops | bytes accessed | tf_op | source)
XLA Modules:
  0.0 61.6 jit_solution(8750924326075029498)
XLA Ops:
  0.0 59.7 %shard_map.64 = f32[1,28,2048]{2,1,0:T(8,128)} custom-call(s32[64]{0:T(128)} %counts.1, s32[64,4,128]{2,1,0:T(4,128)} %token_mask.1, bf16[2,1,128,896]{3,2,1,0:T(8,128)(2,1)} %states.1, bf16[128,2048]{1,0:T(8,128)(2,1)} %queries.1, bf16[128,2048]{1,0:T(8,128)(2,1)} %out_grad.1, bf16[1,896,2048]{2,1,0:T(8,128)(2,1)} %weight.1), custom_call_target="tpu_custom_call" | custom-call | flops 10000000000 | bytes 8000000 | tf_op jit(solution)/shard_map/pallas_call | solution.py:552
  59.7 1.9 %copy.7 = f32[1,28,2048]{2,0,1:T(1,128)} copy(f32[1,28,2048]{2,1,0:T(8,128)} %shard_map.64) | data formatting | bytes 458752 | tf_op jit(solution)/shard_map/pallas_call | solution.py:552
